TPU v7x, 32 devices: a whole 2x2x4 slice. The times are simulated.
32 devices in a mesh: seq: 16 (over z, x, core), batch: 2 (over y).
Axes of the slice: x: 2, y: 2, z: 4, core: 2. Of those that a mesh axis runs over, the one named last changes fastest.
Arguments:
- inputs: bfloat16 [2, 2048, 192], P('batch', 'seq'), may hold values from -6 to 6
- targets: bfloat16 [2, 2048, 192], P('batch', 'seq'), may hold values from -22 to 22
- var_ids: int32 [2, 48], P('batch'), may hold values from 0 to 47, each once within a row
- lead_ids: int32 [2], P('batch'), may hold values from 0 to 31
- block_order: int32 [768], replicated, may hold values from 0 to 767, each once
- blocks: float32 [768, 128, 128], P(('seq', 'batch')), may hold values from -0.1875 to 0.1875
- block_momentum: float32 [768, 128, 128], P(('seq', 'batch'))
- left_stats: float32 [768, 128, 128], P(('seq', 'batch')), as said below
- right_stats: float32 [768, 128, 128], P(('seq', 'batch')), as said below
- left_roots: float32 [768, 128, 128], P(('seq', 'batch')), as said below
- right_roots: float32 [768, 128, 128], P(('seq', 'batch')), as said below
- embed_params: float32 [272, 1024], replicated, may hold values from -3 to 3
- embed_first: float32 [272, 1024], replicated
- embed_second: float32 [272, 1024], replicated
- vectors: float32 [15, 1024], replicated, may hold values from -3 to 3
- vector_first: float32 [15, 1024], replicated
- vector_second: float32 [15, 1024], replicated
- head_weight: float32 [1024, 192], replicated, may hold values from -0.1875 to 0.1875
- head_first: float32 [1024, 192], replicated
- head_second: float32 [1024, 192], replicated
Outputs:
- loss_total: float32 [], replicated
- grad_norm: float32 [], replicated
- new_blocks: float32 [768, 128, 128], P(('seq', 'batch'))
- new_momentum: float32 [768, 128, 128], P(('seq', 'batch'))
- new_left: float32 [768, 128, 128], P(('seq', 'batch'))
- new_right: float32 [768, 128, 128], P(('seq', 'batch'))
- new_embed_first: float32 [272, 1024], replicated
- new_embed_second: float32 [272, 1024], replicated
- new_embed: float32 [272, 1024], replicated
- new_vector_first: float32 [15, 1024], replicated
- new_vector_second: float32 [15, 1024], replicated
- new_vectors: float32 [15, 1024], replicated
- new_head_first: float32 [1024, 192], replicated
- new_head_second: float32 [1024, 192], replicated
- new_head: float32 [1024, 192], replicated
Inputs may be any that keep to these rules, and one draw needn't show every extreme that they name: `var_ids`: each row names each of the 48 variables once. `block_order`: names each of the 768 blocks once. `left_stats`: every block is symmetric. `right_stats`: every block is symmetric. `left_roots`: every block is symmetric. `right_roots`: every block is symmetric.
All inputs are finite; a program needn't handle non-finite values.
Results may differ from a plain program's by a relative error of at most 0.004.
The roundings to bfloat16 on the way count: a program that leaves them out, or rounds other values in their place, can miss the bound.
Values may be sent and summed in bfloat16 or wider, within the bound.
A program may use at most 448 MiB of HBM per device.

v0:
```python
import math

import jax
import jax.numpy as jnp
from jax import lax
from jax.sharding import PartitionSpec as P

D = 1024
HEADS = 16
HD = 64
FF = 4096
VARS = 48
LEADS = 32
LAT_P = 64
KMODES = 32
STEP = 10


HIGH = lax.Precision.HIGHEST
EPS = 1e-05
CLIP_NORM = 0.001
SPECTRAL = 0.5
BETA_ONE = 0.9
BETA_TWO = 0.95
SHAMPOO_RATE = 0.1
DECAY = 0.01
ADAM_EPS = 1e-08
EMBED_RATE = 0.2
VECTOR_RATE = 0.5
HEAD_RATE = 0.05
FLOOR = -1e30


def layer_norm(rows, gain, shift):
    mean = jnp.mean(rows, -1, keepdims=True)
    centred = rows - mean
    return centred * lax.rsqrt(jnp.mean(centred * centred, -1, keepdims=True) + EPS) * gain + shift


def to_blocks(matrix, size):
    rows, cols = matrix.shape
    return (
        matrix.reshape(rows // size, size, cols // size, size)
        .transpose(0, 2, 1, 3)
        .reshape(-1, size, size)
    )


def from_blocks(stack, rows, cols):
    size = stack.shape[-1]
    return (
        stack.reshape(rows // size, cols // size, size, size)
        .transpose(0, 2, 1, 3)
        .reshape(rows, cols)
    )


def split_matrices(stack):
    size = stack.shape[-1]
    found = []
    begin = 0
    for rows, cols in ((D, 3 * D), (D, D), (D, FF), (FF, D)):
        count = rows * cols // (size * size)
        found.append(from_blocks(stack[begin : begin + count], rows, cols))
        begin += count
    return found


def embed_patches(pixels, tok_sel, emb_sel, query, lead_rows):
    tokens = jnp.einsum("spvc,svcd->spvd", pixels, tok_sel, precision=HIGH) + emb_sel[:, None]
    logits = jnp.einsum("spvd,d->spv", tokens, query, precision=HIGH) * (1.0 / math.sqrt(D))
    weights = jax.nn.softmax(logits, -1)
    return jnp.einsum("spv,spvd->spd", weights, tokens, precision=HIGH) + lead_rows[:, None]


def split_heads(rows):
    return rows.reshape(rows.shape[0], rows.shape[1], HEADS, HD)


def attention_forward(query, keys, values):
    seqs, length, _ = query.shape
    scale = 1.0 / math.sqrt(HD)
    heads_q = split_heads(query)
    start_state = (
        jnp.zeros((seqs, HEADS, length, HD), jnp.float32),
        jnp.full((seqs, HEADS, length), FLOOR, jnp.float32),
        jnp.zeros((seqs, HEADS, length), jnp.float32),
    )
    key_rows = lax.all_gather(keys, "seq", axis=1, tiled=True)
    value_rows = lax.all_gather(values, "seq", axis=1, tiled=True)
    count = key_rows.shape[1] // length
    key_blocks = key_rows.reshape(seqs, count, length, HEADS, HD)
    value_blocks = value_rows.reshape(seqs, count, length, HEADS, HD)

    def visit(inner, index):
        acc, top, total = inner
        scores = (
            jnp.einsum(
                "sphd,snhd->shpn", heads_q, key_blocks[:, index], preferred_element_type=jnp.float32
            )
            * scale
        )
        new_top = jnp.maximum(top, jnp.max(scores, -1))
        fade = jnp.exp(top - new_top)
        probs = jnp.exp(scores - new_top[..., None])
        total = total * fade + jnp.sum(probs, -1)
        acc = acc * fade[..., None] + jnp.einsum(
            "shpn,snhd->shpd",
            probs.astype(jnp.bfloat16),
            value_blocks[:, index],
            preferred_element_type=jnp.float32,
        )
        return ((acc, new_top, total), None)

    inner, _ = lax.scan(visit, start_state, jnp.arange(count))
    acc, top, total = inner
    attended = (acc / total[..., None]).transpose(0, 2, 1, 3).reshape(seqs, length, HEADS * HD)
    return (attended, (top + jnp.log(total)).transpose(0, 2, 1))


def attention_backward(query, keys, values, attended, lse, d_att):
    seqs, length, _ = query.shape
    scale = 1.0 / math.sqrt(HD)
    heads_q = split_heads(query)
    heads_k = split_heads(keys)
    heads_v = split_heads(values)
    heads_d = split_heads(d_att)
    delta = jnp.sum(heads_d.astype(jnp.float32) * split_heads(attended), -1)
    lse_h = lse.transpose(0, 2, 1)
    delta_h = delta.transpose(0, 2, 1)
    key_rows = lax.all_gather(keys, "seq", axis=1, tiled=True)
    value_rows = lax.all_gather(values, "seq", axis=1, tiled=True)
    count = key_rows.shape[1] // length
    key_blocks = key_rows.reshape(seqs, count, length, HEADS, HD)
    value_blocks = value_rows.reshape(seqs, count, length, HEADS, HD)

    def visit(inner, index):
        k_part = key_blocks[:, index]
        scores = (
            jnp.einsum("sphd,snhd->shpn", heads_q, k_part, preferred_element_type=jnp.float32)
            * scale
        )
        probs = jnp.exp(scores - lse_h[..., None])
        d_prob = jnp.einsum(
            "sphd,snhd->shpn", heads_d, value_blocks[:, index], preferred_element_type=jnp.float32
        )
        d_score = (probs * (d_prob - delta_h[..., None])).astype(jnp.bfloat16)
        return (
            inner
            + jnp.einsum("shpn,snhd->sphd", d_score, k_part, preferred_element_type=jnp.float32)
            * scale,
            None,
        )

    inner, _ = lax.scan(visit, jnp.zeros((seqs, length, HEADS, HD), jnp.float32), jnp.arange(count))
    d_query = inner
    all_lse, all_delta = (
        lax.all_gather(lse, "seq", axis=1, tiled=True),
        lax.all_gather(delta, "seq", axis=1, tiled=True),
    )
    empty = jnp.zeros((seqs, length, HEADS, HD), jnp.float32)
    q_rows = lax.all_gather(query, "seq", axis=1, tiled=True)
    g_rows = lax.all_gather(d_att, "seq", axis=1, tiled=True)
    count = q_rows.shape[1] // length
    q_blocks = q_rows.reshape(seqs, count, length, HEADS, HD)
    g_blocks = g_rows.reshape(seqs, count, length, HEADS, HD)
    lse_rows = all_lse.reshape(seqs, count, length, HEADS)
    delta_rows = all_delta.reshape(seqs, count, length, HEADS)

    def visit(inner, index):
        d_key, d_value = inner
        q_part = q_blocks[:, index]
        g_part = g_blocks[:, index]
        scores = (
            jnp.einsum("snhd,sphd->shnp", q_part, heads_k, preferred_element_type=jnp.float32)
            * scale
        )
        probs = jnp.exp(scores - lse_rows[:, index].transpose(0, 2, 1)[..., None])
        d_value = d_value + jnp.einsum(
            "shnp,snhd->sphd",
            probs.astype(jnp.bfloat16),
            g_part,
            preferred_element_type=jnp.float32,
        )
        d_prob = jnp.einsum("snhd,sphd->shnp", g_part, heads_v, preferred_element_type=jnp.float32)
        d_score = (probs * (d_prob - delta_rows[:, index].transpose(0, 2, 1)[..., None])).astype(
            jnp.bfloat16
        )
        d_key = (
            d_key
            + jnp.einsum("shnp,snhd->sphd", d_score, q_part, preferred_element_type=jnp.float32)
            * scale
        )
        return ((d_key, d_value), None)

    inner, _ = lax.scan(visit, (empty, empty), jnp.arange(count))
    d_key, d_value = inner
    return (d_query, d_key, d_value)


def feed_inner(normed_two, w_up, vectors):
    upper = jnp.dot(normed_two, w_up, preferred_element_type=jnp.float32) + vectors[11:].reshape(-1)
    return (upper, jax.nn.gelu(upper).astype(jnp.bfloat16))


def layer_forward(rows, seqs, mats, vectors):
    w_qkv, w_out, w_up, w_down = mats
    normed = layer_norm(rows, vectors[1], vectors[2]).astype(jnp.bfloat16)
    bias = jnp.concatenate([vectors[9], jnp.zeros_like(vectors[9]), vectors[10]])
    qkv = (jnp.dot(normed, w_qkv, preferred_element_type=jnp.float32) + bias).astype(jnp.bfloat16)
    query = qkv[:, :D].reshape(seqs, -1, D)
    keys = qkv[:, D : 2 * D].reshape(seqs, -1, D)
    values = qkv[:, 2 * D :].reshape(seqs, -1, D)
    attended, lse = attention_forward(query, keys, values)
    att_low = attended.reshape(-1, D).astype(jnp.bfloat16)
    mid = rows + jnp.dot(att_low, w_out, preferred_element_type=jnp.float32) + vectors[7]
    normed_two = layer_norm(mid, vectors[3], vectors[4]).astype(jnp.bfloat16)
    upper, active = feed_inner(normed_two, w_up, vectors)
    out = mid + jnp.dot(active, w_down, preferred_element_type=jnp.float32) + vectors[8]
    saved = (upper, active)
    return (out, (rows, normed, query, keys, values, attended, lse, mid, normed_two, saved))


def layer_backward(d_out, kept, mats, vectors):
    rows, normed, query, keys, values, attended, lse, mid, normed_two, saved = kept
    w_qkv, w_out, w_up, w_down = mats
    upper, active = saved
    d_branch = d_out.astype(jnp.bfloat16)
    g_down = jnp.einsum("rf,rd->fd", active, d_branch, preferred_element_type=jnp.float32)
    d_active = jnp.einsum("rd,fd->rf", d_branch, w_down, preferred_element_type=jnp.float32)
    d_upper = jax.vjp(jax.nn.gelu, upper)[1](d_active)[0].astype(jnp.bfloat16)
    g_up = jnp.einsum("rd,rf->df", normed_two, d_upper, preferred_element_type=jnp.float32)
    d_normed_two = jnp.einsum("rf,df->rd", d_upper, w_up, preferred_element_type=jnp.float32)
    d_mid_norm, g_gain_two, g_shift_two = jax.vjp(layer_norm, mid, vectors[3], vectors[4])[1](
        d_normed_two
    )
    d_mid = d_out + d_mid_norm
    d_mid_low = d_mid.astype(jnp.bfloat16)
    att_low = attended.reshape(-1, D).astype(jnp.bfloat16)
    g_out = jnp.einsum("ra,rd->ad", att_low, d_mid_low, preferred_element_type=jnp.float32)
    d_att = jnp.einsum("rd,ad->ra", d_mid_low, w_out, preferred_element_type=jnp.float32).astype(
        jnp.bfloat16
    )
    seqs = query.shape[0]
    d_query, d_key, d_value = attention_backward(
        query, keys, values, attended, lse, d_att.reshape(seqs, -1, D)
    )
    d_qkv = jnp.concatenate(
        [d_query.reshape(-1, D), d_key.reshape(-1, D), d_value.reshape(-1, D)], 1
    ).astype(jnp.bfloat16)
    g_qkv = jnp.einsum("rd,re->de", normed, d_qkv, preferred_element_type=jnp.float32)
    d_normed = jnp.einsum("re,de->rd", d_qkv, w_qkv, preferred_element_type=jnp.float32)
    d_rows_norm, g_gain_one, g_shift_one = jax.vjp(layer_norm, rows, vectors[1], vectors[2])[1](
        d_normed
    )
    qkv_sums = jnp.sum(d_qkv.astype(jnp.float32), 0)
    small = (
        g_gain_one,
        g_shift_one,
        g_gain_two,
        g_shift_two,
        jnp.sum(d_mid_low.astype(jnp.float32), 0),
        jnp.sum(d_branch.astype(jnp.float32), 0),
        qkv_sums[:D],
        qkv_sums[2 * D :],
        jnp.sum(d_upper.astype(jnp.float32), 0),
    )
    return (d_mid + d_rows_norm, (g_qkv, g_out, g_up, g_down), small)


def loss_terms(pred, targets, seqs, length):
    strips = lax.axis_size("seq")
    cols = length // LAT_P
    nlat = 2 * LAT_P
    nlon = 2 * cols * strips
    all_seqs = seqs * lax.axis_size("batch")
    diff = pred.reshape(seqs, length, -1) - targets.astype(jnp.float32)
    grid = (
        diff.reshape(seqs, cols, LAT_P, VARS, 2, 2)
        .transpose(0, 3, 2, 4, 1, 5)
        .reshape(seqs, VARS, nlat, 2 * cols)
    )
    lat = ((jnp.arange(nlat, dtype=jnp.float32) + 0.5) / nlat - 0.5) * math.pi
    weight = jnp.cos(lat)
    weight = (weight / jnp.mean(weight))[None, None, :, None]
    column = lax.axis_index("seq") * (2 * cols) + jnp.arange(2 * cols, dtype=jnp.int32)
    modes = jnp.arange(KMODES, dtype=jnp.int32)
    angle = (column[:, None] * modes[None] % nlon).astype(jnp.float32) * (2.0 * math.pi / nlon)
    cosine = jnp.cos(angle)
    sine = jnp.sin(angle)
    part_c = jnp.einsum("svrc,ck->svrk", grid, cosine, precision=HIGH)
    part_s = jnp.einsum("svrc,ck->svrk", grid, sine, precision=HIGH)
    full_c, full_s = lax.psum((part_c, part_s), "seq")
    mse_count = all_seqs * VARS * nlat * nlon
    dft_count = nlon * all_seqs * VARS * nlat * KMODES
    mse = jnp.sum(weight * grid * grid) / mse_count
    spectral = SPECTRAL * jnp.sum(weight * (full_c * full_c + full_s * full_s)) / dft_count
    first = (lax.axis_index("seq") == 0).astype(jnp.float32)
    back_wave = jnp.einsum("svrk,ck->svrc", full_c, cosine, precision=HIGH) + jnp.einsum(
        "svrk,ck->svrc", full_s, sine, precision=HIGH
    )
    d_grid = 2.0 * weight * grid / mse_count + 2.0 * SPECTRAL / dft_count * weight * back_wave
    d_pred = (
        d_grid.reshape(seqs, VARS, LAT_P, 2, cols, 2)
        .transpose(0, 4, 2, 1, 3, 5)
        .reshape(seqs * length, VARS * 4)
    )
    return (d_pred, mse + first * spectral)


def adam(value, first, second, grad, rate):
    first = BETA_ONE * first + (1.0 - BETA_ONE) * grad
    second = BETA_TWO * second + (1.0 - BETA_TWO) * grad * grad
    step = first / (1.0 - BETA_ONE**STEP) / (jnp.sqrt(second / (1.0 - BETA_TWO**STEP)) + ADAM_EPS)
    return (first, second, value - rate * (step + DECAY * value))


def shards(
    inputs,
    targets,
    var_ids,
    lead_ids,
    block_order,
    blocks,
    block_momentum,
    left_stats,
    right_stats,
    left_roots,
    right_roots,
    embed_params,
    embed_first,
    embed_second,
    vectors,
    vector_first,
    vector_second,
    head_weight,
    head_first,
    head_second,
):
    seqs, length, _ = inputs.shape
    size = blocks.shape[-1]
    low_blocks = blocks.astype(jnp.bfloat16)
    stack = lax.all_gather(low_blocks, ("seq", "batch"), axis=0, tiled=True)
    natural = jnp.zeros_like(stack).at[block_order].set(stack)
    mats = split_matrices(natural)
    head_low = head_weight.astype(jnp.bfloat16)
    pick = (var_ids[..., None] == jnp.arange(VARS, dtype=jnp.int32)[None, None]).astype(jnp.float32)
    lead_pick = (lead_ids[:, None] == jnp.arange(LEADS, dtype=jnp.int32)[None]).astype(jnp.float32)
    tok_sel = jnp.einsum(
        "svw,wcd->svcd", pick, embed_params[: VARS * 4].reshape(VARS, 4, D), precision=HIGH
    )
    emb_sel = jnp.einsum("svw,wd->svd", pick, embed_params[VARS * 4 : VARS * 5], precision=HIGH)
    lead_rows = jnp.dot(lead_pick, embed_params[VARS * 5 :], precision=HIGH)
    pixels = inputs.astype(jnp.float32).reshape(seqs, length, VARS, 4)

    def embed_local(tok_part, emb_part, query, lead_part):
        return embed_patches(pixels, tok_part, emb_part, query, lead_part)

    stream, embed_back = jax.vjp(embed_local, tok_sel, emb_sel, vectors[0], lead_rows)
    out, kept = layer_forward(stream.reshape(-1, D), seqs, mats, vectors)
    final_rows, final_back = jax.vjp(layer_norm, out, vectors[5], vectors[6])
    final = final_rows.astype(jnp.bfloat16)
    pred = jnp.dot(final, head_low, preferred_element_type=jnp.float32)
    d_pred, loss_part = loss_terms(pred, targets, seqs, length)
    d_low = d_pred.astype(jnp.bfloat16)
    g_head = jnp.einsum("rd,ro->do", final, d_low, preferred_element_type=jnp.float32)
    d_final = jnp.einsum("ro,do->rd", d_low, head_low, preferred_element_type=jnp.float32)
    d_out, g_gain_final, g_shift_final = final_back(d_final)
    d_rows, matrix_grads, small = layer_backward(d_out, kept, mats, vectors)
    d_tok, d_emb, d_query, d_lead = embed_back(d_rows.reshape(seqs, length, D))
    g_embed = jnp.concatenate(
        [
            jnp.einsum("svw,svcd->wcd", pick, d_tok, precision=HIGH).reshape(VARS * 4, D),
            jnp.einsum("svw,svd->wd", pick, d_emb, precision=HIGH),
            jnp.einsum("sl,sd->ld", lead_pick, d_lead, precision=HIGH),
        ]
    )
    g_gain_one, g_shift_one, g_gain_two, g_shift_two, b_out, b_down, b_query, b_value, b_up = small
    g_vectors = jnp.concatenate(
        [
            jnp.stack(
                [
                    d_query,
                    g_gain_one,
                    g_shift_one,
                    g_gain_two,
                    g_shift_two,
                    g_gain_final,
                    g_shift_final,
                    b_out,
                    b_down,
                    b_query,
                    b_value,
                ]
            ),
            b_up.reshape(-1, D),
        ]
    )
    slot_grads = jnp.concatenate([to_blocks(grad, size) for grad in matrix_grads])[block_order]
    owned = lax.psum_scatter(slot_grads, ("seq", "batch"), scatter_dimension=0, tiled=True)
    g_embed, g_vectors, g_head, loss_total = lax.psum(
        (g_embed, g_vectors, g_head, loss_part), ("seq", "batch")
    )
    rest_squares = (
        jnp.sum(g_embed * g_embed) + jnp.sum(g_vectors * g_vectors) + jnp.sum(g_head * g_head)
    )
    grad_norm = jnp.sqrt(lax.psum(jnp.sum(owned * owned), ("seq", "batch")) + rest_squares)
    clip = CLIP_NORM / jnp.maximum(grad_norm, CLIP_NORM)
    owned = owned * clip
    new_momentum = BETA_ONE * block_momentum + (1.0 - BETA_ONE) * owned
    new_left = BETA_TWO * left_stats + (1.0 - BETA_TWO) * jnp.einsum(
        "bij,bkj->bik", owned, owned, precision=HIGH
    )
    new_right = BETA_TWO * right_stats + (1.0 - BETA_TWO) * jnp.einsum(
        "bji,bjk->bik", owned, owned, precision=HIGH
    )
    direction = jnp.einsum(
        "bij,bjk->bik",
        jnp.einsum("bij,bjk->bik", left_roots, new_momentum, precision=HIGH),
        right_roots,
        precision=HIGH,
    )
    new_blocks = blocks - SHAMPOO_RATE * (direction + DECAY * blocks)
    e_one, e_two, e_new = adam(embed_params, embed_first, embed_second, g_embed * clip, EMBED_RATE)
    v_one, v_two, v_new = adam(vectors, vector_first, vector_second, g_vectors * clip, VECTOR_RATE)
    h_one, h_two, h_new = adam(head_weight, head_first, head_second, g_head * clip, HEAD_RATE)
    return (
        loss_total,
        grad_norm,
        new_blocks,
        new_momentum,
        new_left,
        new_right,
        e_one,
        e_two,
        e_new,
        v_one,
        v_two,
        v_new,
        h_one,
        h_two,
        h_new,
    )


def solution(mesh):
    in_specs = (
        P("batch", "seq", None),
        P("batch", "seq", None),
        P("batch", None),
        P("batch"),
        P(),
        P(("seq", "batch"), None, None),
        P(("seq", "batch"), None, None),
        P(("seq", "batch"), None, None),
        P(("seq", "batch"), None, None),
        P(("seq", "batch"), None, None),
        P(("seq", "batch"), None, None),
        P(),
        P(),
        P(),
        P(),
        P(),
        P(),
        P(),
        P(),
        P(),
    )
    out_specs = (
        P(),
        P(),
        P(("seq", "batch"), None, None),
        P(("seq", "batch"), None, None),
        P(("seq", "batch"), None, None),
        P(("seq", "batch"), None, None),
        P(),
        P(),
        P(),
        P(),
        P(),
        P(),
        P(),
        P(),
        P(),
    )
    return jax.shard_map(shards, mesh=mesh, in_specs=in_specs, out_specs=out_specs, check_vma=False)
```

profile of v0, /device:TPU:0, one launch (start us, length us, event | category | flops | bytes accessed | tf_op | source)
XLA Modules:
  0.0 1750.9 jit_solution(9103725415910378037)
XLA Ops:
  14.3 20.1 %fusion.156 = f32[48,1024,128]{2,1,0:T(8,128)S(1)} fusion(bf16[128,48,4]{0,2,1:T(4,128)(2,1)S(1)} %bitcast.551, f32[48,4,1024]{2,0,1:T(8,128)S(1)} %fusion.158), kind=kOutput, calls=%fused_computation.170 | convolution fusion | flops 301989888 | bytes 26001408 | tf_op jit(solution)/shard_map/jvp(spvc,svcd->spvd)/dot_general | solution.py:70
  34.5 17.4 fusion.70
  63.5 105.4 %all-gather.11.cloned.1.call-done = bf16[768,128,128]{2,1,0:T(8,128)(2,1)} async-done(((bf16[24,128,128]{2,1,0:T(8,128)(2,1)}), bf16[768,128,128]{2,1,0:T(8,128)(2,1)}) %all-gather.11.cloned.1.call-update) | async-done | bytes 25165840 | tf_op jit(solution)/shard_map/all_gather | solution.py:343
  177.8 112.6 %scatter_fusion = bf16[768,128,128]{2,1,0:T(8,128)(2,1)} fusion(bf16[768,128,128]{2,1,0:T(8,128)(2,1)} %broadcast_in_dim.45, s32[768]{0:T(1024)S(1)} %compare_select_fusion, bf16[768,128,128]{2,1,0:T(8,128)(2,1)} %all-gather.11.cloned.1.call-done), kind=kCustom, calls=%fused_computation.1 | custom fusion | bytes 75500544 | tf_op jit(solution)/shard_map/scatter | solution.py:344
  308.8 12.3 fusion.234
  321.1 12.1 copy.181
  333.2 23.1 %copy.182 = bf16[32,8,128,128]{3,1,2,0:T(8,128)(2,1)} copy(bf16[32,8,128,128]{3,2,1,0:T(8,128)(2,1)} %bitcast.482) | data formatting | bytes 16777216 | tf_op jit(solution)/shard_map/reshape | solution.py:52
  356.6 11.9 reshape.781
  378.8 24.2 %all-gather.15.cloned.1.call-done = bf16[2048,1024]{1,0:T(8,128)(2,1)} async-done(((bf16[128,1024]{1,0:T(8,128)(2,1)}), bf16[2048,1024]{1,0:T(8,128)(2,1)}) %all-gather.15.cloned.1.call-update) | async-done | bytes 4194320 | tf_op jit(solution)/shard_map/all_gather | solution.py:90
  403.0 11.7 reshape.782
  425.0 85.5 %while.39 = (s32[]{:T(128)}, f32[1,16,128,64]{2,3,1,0:T(8,128)S(1)}, f32[1,16,128]{2,1,0:T(8,128)S(1)}, f32[1,16,128]{2,1,0:T(8,128)S(1)}, s32[16]{0:T(128)S(1)}...) while((s32[]{:T(128)}, ...), condition=%wide.region_9.10_spmd.clone, body=%wide.region_6.9_spmd.clone.sunk | while | flops 69087232 | bytes 5111991 | solution.py:115
  563.6 19.4 %all_gather.27 = f32[1,2048,16]{1,2,0:T(8,128)S(1)} all-gather(f32[1,128,16]{1,2,0:T(8,128)S(1)} %bitcast.528), channel_id=1, replica_groups=mesh['seq'=16,'batch'=2] {'seq'}, dimensions={1}, use_global_device_ids=true | all-gather | bytes 139264 | tf_op jit(solution)/shard_map/all_gather | solution.py:158
  583.6 42.3 %all-reduce.8.cloned.1.call-done = (f32[1,48,128,32]{2,3,1,0:T(8,128)}, f32[1,48,128,32]{2,3,1,0:T(8,128)}) async-done(((f32[1,48,128,32]{2,3,1,0:T(8,128)}, f32[1,48,128,32]{2,3,1,0:T(8,128)}), (f32[1,48,128,32]{2,3,1,0:T(8,128)}, f32[1,48,128,32]{2,3,1,0:T(8,128)})) %all-reduce.8.cloned.1.call-update) | async-done | bytes 1572880 | tf_op jit(solution)/shard_map/psum | solution.py:293
  659.8 102.7 %while.40 = (s32[]{:T(128)}, f32[1,128,16,64]{1,3,2,0:T(8,128)}, s32[16]{0:T(128)S(1)}, bf16[1,16,128,16,64]{2,4,3,1,0:T(8,128)(2,1)}, bf16[1,128,16,64]{1,3,2,0...) while((s32[]{:T(128)}, f32[1,128,16,64]{1,3,2,0:T(8,128)}, ...), condition=%wide.region_25.26_spmd.clone, body=%wide.region_24.25_spmd.clone.sunk | while | flops 102367232 | bytes 4474552 | solution.py:155
  764.3 19.8 %all-gather.4 = f32[2048,16]{0,1:T(8,128)S(1)} all-gather(f32[128,16]{0,1:T(8,128)S(1)} %bitcast.527), channel_id=6, replica_groups=mesh['seq'=16,'batch'=2] {'seq'}, dimensions={0}, use_global_device_ids=true | all-gather | bytes 139264 | tf_op jit(solution)/shard_map/all_gather | solution.py:159
  805.5 11.8 copy.202
  843.1 170.2 %while.41 = (s32[]{:T(128)}, f32[1,128,16,64]{1,3,2,0:T(8,128)}, f32[1,128,16,64]{1,3,2,0:T(8,128)}, s32[16]{0:T(128)S(1)}, bf16[1,16,128,16,64]{2,4,3,1,0:T(8,1...) while((s32[]{:T(128)}, f32[1,128,16,64]{1,3,2,0:T(8,128)}, ...), condition=%wide.region_27.28_spmd.clone, body=%wide.region_26.27_spmd.clone.sunk | while | flops 136445952 | bytes 6866637 | solution.py:196
  1041.6 59.6 %fusion.124 = f32[48,4,1024]{2,1,0:T(4,128)S(1)} fusion(bf16[128,48,4]{0,2,1:T(4,128)(2,1)S(1)} %bitcast.552, f32[1024]{0:T(1024)S(1)} %bitcast.560, f32[128,48]{0,1:T(8,128)S(1)} %multiply_multiply_fusion.6, f32[128,48]{0,1:T(8,128)S(1)} %copy-done.51, f32[128,1024]{0,1:T(8,128)S(1)} %copy.204), kind=kOutput, calls=%fused_computation.144 | convolution fusion | flops 320864256 | bytes 1413120 | tf_op jit(solution)/shard_map/transpose(jvp(spvc,svcd->spvd))/dot_general | solution.py:70
  1112.8 35.1 %pad_maximum_fusion = f32[768,128,128]{2,1,0:T(8,128)} fusion(f32[256,128,128]{2,1,0:T(8,128)} %bitcast.479, f32[256,128,128]{2,1,0:T(8,128)} %bitcast.480, f32[64,128,128]{2,1,0:T(8,128)} %bitcast.486, f32[192,128,128]{2,1,0:T(8,128)} %bitcast.481), kind=kLoop, calls=%fused_computation.73 | loop fusion | flops 37748736 | bytes 100663296 | tf_op jit(solution)/shard_map/concatenate | solution.py:399
  1147.9 35.6 %gather_fusion = f32[768,128,128]{2,1,0:T(8,128)} fusion(f32[768,128,128]{2,1,0:T(8,128)} %pad_maximum_fusion, s32[1024]{0:T(1024)S(1)} %copy-done.64), kind=kCustom, calls=%fused_computation | custom fusion | bytes 100666368 | tf_op jit(solution)/shard_map/gather | solution.py:399
  1188.1 27.5 %fusion.147 = f32[1,1024]{1,0:T(1,128)S(1)} fusion(f32[128,48,1]{0,2,1:T(1,128)S(1)} %bitcast.530, f32[48,1024,128]{2,1,0:T(8,128)} %copy-done.1, f32[48,1024]{1,0:T(8,128)S(1)} %copy-done.11), kind=kOutput, calls=%fused_computation.162 | convolution fusion | flops 81788928 | bytes 25391104 | tf_op jit(solution)/shard_map/transpose(jvp(spvd,d->spv))/dot_general | solution.py:71
  1215.9 19.8 %all-reduce.6.cloned.1.call-done = (f32[272,1024]{1,0:T(8,128)}, f32[1024,192]{0,1:T(8,128)}) async-done(((f32[272,1024]{1,0:T(8,128)}, f32[1024,192]{0,1:T(8,128)}), (f32[272,1024]{1,0:T(8,128)}, f32[1024,192]{0,1:T(8,128)})) %all-reduce.6.cloned.1.call-update) | async-done | bytes 1900560 | tf_op jit(solution)/shard_map/psum | solution.py:401
  1237.8 435.3 %reduce-scatter.2.cloned.1.call-done = f32[24,128,128]{2,1,0:T(8,128)} async-done(((f32[768,128,128]{2,1,0:T(8,128)}), f32[24,128,128]{2,1,0:T(8,128)}) %reduce-scatter.2.cloned.1.call-update) | async-done | bytes 1572880 | tf_op jit(solution)/shard_map/reduce_scatter | solution.py:400
  1677.6 39.9 %all-reduce = (f32[]{:T(128)}, f32[]{:T(128)}, f32[15,1024]{1,0:T(8,128)S(1)}) all-reduce(f32[]{:T(128)S(6)} %add.394, f32[]{:T(128)} %multiply_reduce_fusion, f32[15,1024]{1,0:T(8,128)S(1)} %concatenate.20), channel_id=1, replica_groups=mesh['seq'=16,'batch'=2] {'seq','batch'}, use_global_device_ids=true, to_apply=%region_18.19 | all-reduce | flops 15362 | bytes 122896 | tf_op jit(solution)/shard_map/psum | solution.py:401
  (617 shorter events, 536.9 us)
Async XLA Ops:
  7.2 1716.0 %copy-start = (f32[24,128,128]{2,1,0:T(8,128)S(1)}, f32[24,128,128]{2,1,0:T(8,128)}, u32[]{:S(2)}) copy-start(f32[24,128,128]{2,1,0:T(8,128)} %param.35) | copy-start | bytes 4718596
  7.2 161.7 %all-gather.11.cloned.1.call-start = ((), (), s32[]{:S(2)}) async-start(), calls=%async_computation.1 | async-start | bytes 25952256 | tf_op jit(solution)/shard_map/all_gather | solution.py:343
  9.9 346.8 %all-gather.13.cloned.1.call-start = ((), (), s32[]{:S(2)}) async-start(), calls=%async_computation.3 | async-start | bytes 4456448 | tf_op jit(solution)/shard_map/all_gather | solution.py:89
  12.1 39.9 %copy-start.10 = (f32[48,1024]{1,0:T(8,128)}, f32[48,1024]{1,0:T(8,128)S(1)}, u32[]{:S(2)}) copy-start(f32[48,1024]{1,0:T(8,128)S(1)} %fusion.171) | copy-start | bytes 589828
  63.0 240.5 %copy-start.57 = (f32[1,1024]{1,0:T(1,128)}, f32[1,1024]{1,0:T(1,128)S(1)}, u32[]{:S(2)}) copy-start(f32[1,1024]{1,0:T(1,128)S(1)} %get-tuple-element.501) | copy-start | bytes 12292
  63.3 240.2 %copy-start.78 = (f32[128]{0:T(128)}, f32[128]{0:T(128)S(1)}, u32[]{:S(2)}) copy-start(f32[128]{0:T(128)S(1)} %broadcast_multiply_fusion.5) | copy-start | bytes 1540
  63.5 114.3 %copy-start.88 = (f32[128]{0:T(128)}, f32[128]{0:T(128)S(1)}, u32[]{:S(2)}) copy-start(f32[128]{0:T(128)S(1)} %multiply_reduce_fusion.12) | copy-start | bytes 1540
  63.5 240.0 %copy-start.85 = (f32[128]{0:T(128)}, f32[128]{0:T(128)S(1)}, u32[]{:S(2)}) copy-start(f32[128]{0:T(128)S(1)} %fusion.205) | copy-start | bytes 1540
  302.1 54.3 %copy-start.30 = (bf16[128,1024]{1,0:T(8,128)(2,1)}, bf16[128,1024]{1,0:T(8,128)(2,1)S(1)}, u32[]{:S(2)}) copy-start(bf16[128,1024]{1,0:T(8,128)(2,1)S(1)} %get-tuple-element.490) | copy-start | bytes 786436
  302.1 100.9 %all-gather.15.cloned.1.call-start = ((), (), s32[]{:S(2)}) async-start(), calls=%async_computation.4 | async-start | bytes 4456448 | tf_op jit(solution)/shard_map/all_gather | solution.py:90
  302.9 238.8 %all-gather.17.cloned.1.call-start = ((), (), s32[]{:S(2)}) async-start(), calls=%async_computation.5 | async-start | bytes 4456448 | tf_op jit(solution)/shard_map/all_gather | solution.py:162
  356.6 269.4 %all-reduce.8.cloned.1.call-start = ((), (), s32[]{:S(2)}) async-start(), calls=%async_computation.8 | async-start | bytes 3145728 | tf_op jit(solution)/shard_map/psum | solution.py:293
  521.8 129.7 %copy-start.3 = (f32[128,1024]{1,0:T(8,128)}, f32[128,1024]{1,0:T(8,128)S(1)}, u32[]{:S(2)}) copy-start(f32[128,1024]{1,0:T(8,128)S(1)} %get-tuple-element.508) | copy-start | bytes 1572868
  531.5 289.6 %all-gather.19.cloned.1.call-start = ((), (), s32[]{:S(2)}) async-start(), calls=%async_computation.6 | async-start | bytes 4456448 | tf_op jit(solution)/shard_map/all_gather | solution.py:163
  654.9 580.8 %all-reduce.6.cloned.1.call-start = ((), (), s32[]{:S(2)}) async-start(), calls=%async_computation.7 | async-start | bytes 3801088 | tf_op jit(solution)/shard_map/psum | solution.py:401
  1034.8 66.4 %copy-start.48 = (f32[128,48]{0,1:T(8,128)}, f32[128,48]{0,1:T(8,128)S(1)}, u32[]{:S(2)}) copy-start(f32[128,48]{0,1:T(8,128)S(1)} %multiply_multiply_fusion.6) | copy-start | bytes 73732
  1041.6 59.7 %copy-start.73 = (s32[1,48]{1,0:T(1,128)S(1)}, s32[1,48]{1,0:T(1,128)}, u32[]{:S(2)}) copy-start(s32[1,48]{1,0:T(1,128)} %param.28) | copy-start | bytes 580
  1105.3 567.8 %reduce-scatter.2.cloned.1.call-start = ((), (), s32[]{:S(2)}) async-start(), calls=%async_computation.2 | async-start | bytes 51904512 | tf_op jit(solution)/shard_map/reduce_scatter | solution.py:400
  1112.8 35.1 %copy-start.64 = (s32[1024]{0:T(1024)S(1)}, s32[1024]{0:T(1024)}, u32[]{:S(2)}) copy-start(s32[1024]{0:T(1024)} %pad_clamp_fusion) | copy-start | bytes 12292
  1188.0 27.7 %copy-start.60 = (f32[1024]{0:T(1024)S(1)}, f32[1024]{0:T(1024)}, u32[]{:S(2)}) copy-start(f32[1024]{0:T(1024)} %get-tuple-element.392) | copy-start | bytes 12292
  1215.7 505.1 %copy-start.47 = (f32[15,1024]{1,0:T(8,128)S(1)}, f32[15,1024]{1,0:T(8,128)}, u32[]{:S(2)}) copy-start(f32[15,1024]{1,0:T(8,128)} %param.40) | copy-start | bytes 184324
  1215.7 505.1 %copy-start.54 = (f32[15,1024]{1,0:T(8,128)S(1)}, f32[15,1024]{1,0:T(8,128)}, u32[]{:S(2)}) copy-start(f32[15,1024]{1,0:T(8,128)} %param.42) | copy-start | bytes 184324
  1215.7 505.1 %copy-start.55 = (f32[15,1024]{1,0:T(8,128)S(1)}, f32[15,1024]{1,0:T(8,128)}, u32[]{:S(2)}) copy-start(f32[15,1024]{1,0:T(8,128)} %param.41) | copy-start | bytes 184324
  1673.1 48.4 %copy-start.2 = (f32[24,128,128]{2,1,0:T(8,128)S(1)}, f32[24,128,128]{2,1,0:T(8,128)}, u32[]{:S(2)}) copy-start(f32[24,128,128]{2,1,0:T(8,128)} %reduce-scatter.2.cloned.1.call-done) | copy-start | bytes 4718596
  (83 other events, 673.6 us)
Sparse Core Ops, SparseCore 0:
  11.5 157.3 all-gather.10
  302.2 48.8 all-gather.12
  353.9 49.0 all-gather.14
  405.0 49.0 all-gather.16
  531.6 94.2 all-reduce.7
  655.0 49.6 all-gather.18
  1105.4 130.2 all-reduce.5
  1242.1 430.9 reduce-scatter.1
where the time goes:
time: 1770 us; the launch traced here: 1750 us
  waiting for transfers between devices  628 us (35%)
  local copies, waits for them, and re-layouts  416 us (24%)
  matrix products  409 us (23%)
  other arithmetic  102 us (6%)
  loops' own time  94.8 us (5%)
  blocking collectives  79.1 us (4%)
  between operations  22.3 us (1%)
    reduce_scatter x1, waiting for transfers between devices, shards(): lax.psum_scatter(slot_grads, ('seq', 'batch'), scatter_dimension=0, tiled...  435 us
    scatter x1, local copies, waits for them, and re-layouts, shards(): natural = jnp.zeros_like(stack).at[block_order].set(stack)  113 us
    all_gather x1, waiting for transfers between devices, shards(): stack = lax.all_gather(low_blocks, ('seq', 'batch'), axis=0, tiled=True)  105 us
    dot_general x2, matrix products, embed_patches(): jnp.einsum('spvc,svcd->spvd', pixels, tok_sel, precision=HIGH)  79.8 us
    unnamed x206, local copies, waits for them, and re-layouts  55.6 us
    dot_general x2, matrix products, embed_patches(): jnp.einsum('spvd,d->spv', tokens, query, precision=HIGH)  44.9 us
    dot_general x16, matrix products, visit(): jnp.einsum('shnp,snhd->sphd', d_score, q_part, preferred_element_type=jnp...  42.4 us
    psum x1, waiting for transfers between devices, loss_terms(): full_c, full_s = lax.psum((part_c, part_s), 'seq')  42.3 us
  transfers between devices with their start and end apart: 8, of which 5 were waited for; matrix products, arithmetic and copies ran while one was open for 27% of the time, Pallas kernels for 0%

commit v1 on v0

--- a/solution.py
+++ b/solution.py
@@ -3,6 +3,8 @@
 import jax
 import jax.numpy as jnp
 from jax import lax
+from jax.experimental import pallas as pl
+from jax.experimental.pallas import tpu as pltpu
 from jax.sharding import PartitionSpec as P
 
 D = 1024
@@ -29,6 +31,10 @@
 VECTOR_RATE = 0.5
 HEAD_RATE = 0.05
 FLOOR = -1e30
+EROWS = VARS * 5 + LEADS
+HOUT = VARS * 4
+MSE_COUNT = 786432.0
+DFT_COUNT = 25165824.0
 
 
 def layer_norm(rows, gain, shift):
@@ -443,6 +449,710 @@
     )
 
 
+TOK = 128
+NSEQ = 16
+BLOCK = 128
+N_LEFT = 56
+N_RIGHT = 72
+QCH = 256
+LOG2E = math.log2(math.e)
+MESH_ID = pl.DeviceIdType.MESH
+NT = (((1,), (1,)), ((), ()))
+TN = (((0,), (0,)), ((), ()))
+NN = (((1,), (0,)), ((), ()))
+BF = jnp.bfloat16
+F32 = jnp.float32
+VM = pltpu.VMEM
+
+
+def mm(a, b, dims=NN):
+    return lax.dot_general(a, b, dims, preferred_element_type=F32)
+
+
+def mmh(a, b, dims=NN):
+    return lax.dot_general(a, b, dims, precision=HIGH, preferred_element_type=F32)
+
+
+def flip(x):
+    return jnp.swapaxes(x.astype(F32), 0, 1).astype(x.dtype)
+
+
+def normalise(x):
+    mean = jnp.mean(x, -1, keepdims=True)
+    centred = x - mean
+    rstd = lax.rsqrt(jnp.mean(centred * centred, -1, keepdims=True) + EPS)
+    return centred * rstd, rstd
+
+
+def normalise_back(grad, unit, rstd, gain):
+    inner = grad * gain
+    return rstd * (
+        inner
+        - jnp.mean(inner, -1, keepdims=True)
+        - unit * jnp.mean(inner * unit, -1, keepdims=True)
+    )
+
+
+def column_sum(x):
+    return jnp.sum(x, 0, keepdims=True)
+
+
+GELU_K = math.sqrt(2.0 / math.pi)
+
+
+def gelu_value(x):
+    return 0.5 * x * (1.0 + jnp.tanh(GELU_K * (x + 0.044715 * x * x * x)))
+
+
+def gelu_slope(x):
+    t = jnp.tanh(GELU_K * (x + 0.044715 * x * x * x))
+    return 0.5 * (1.0 + t) + 0.5 * x * (1.0 - t * t) * GELU_K * (1.0 + 3.0 * 0.044715 * x * x)
+
+
+def layer_kernel(
+    n1_ref,
+    h0_ref,
+    vec_ref,
+    bias_ref,
+    bup_ref,
+    goal_ref,
+    head_ref,
+    wlat_ref,
+    wqkv_hbm,
+    wo_hbm,
+    wup_hbm,
+    wdown_hbm,
+    left_hbm,
+    right_hbm,
+    drow_ref,
+    gvec_ref,
+    gup_ref,
+    ghead_ref,
+    loss_ref,
+    wqkv,
+    wo,
+    wup,
+    wdown,
+    left,
+    right,
+    slab,
+    qkv_t,
+    out_t,
+    out_t32,
+    lse,
+    o_in,
+    d_slab,
+    do_t,
+    dqkv_t,
+    dqkv_in,
+    k_row,
+    v_row,
+    q_row,
+    do_row,
+    s_scr,
+    dk_acc,
+    dv_acc,
+    mid_s,
+    up_s,
+    acc,
+    wave,
+    w_sem,
+    a_send,
+    a_recv,
+    x_send,
+    x_recv,
+    g_local,
+    g_send,
+    g_recv,
+):
+    s = lax.axis_index("seq")
+    b = lax.axis_index("batch")
+    core = lax.rem(s, 2)
+    xpos = lax.rem(s // 2, 2)
+    zpos = s // 4
+    sibling = s + 1 - 2 * core
+
+    copies = []
+    for i, (src, dst) in enumerate(((wqkv_hbm, wqkv), (wo_hbm, wo), (wup_hbm, wup), (wdown_hbm, wdown))):
+        c = pltpu.make_async_copy(src, dst, w_sem.at[i])
+        c.start()
+        copies.append(c)
+
+    barrier = pltpu.get_barrier_semaphore()
+
+    def greet(o, _):
+        pl.semaphore_signal(
+            barrier, inc=1, device_id=(lax.rem(s + o, NSEQ), b), device_id_type=MESH_ID
+        )
+        return _
+
+    lax.fori_loop(1, NSEQ, greet, 0)
+    pl.semaphore_wait(barrier, NSEQ - 1)
+
+    share = []
+
+    def share_group(index, stage, target, begin, count):
+        part = pl.ds(begin, count)
+        c = pltpu.make_async_copy(stage.at[part], target.at[0, part], g_local.at[index])
+        c.start()
+        r = pltpu.make_async_remote_copy(
+            src_ref=stage.at[part],
+            dst_ref=target.at[1, part],
+            send_sem=g_send.at[index],
+            recv_sem=g_recv.at[index],
+            device_id=(sibling, b),
+            device_id_type=MESH_ID,
+        )
+        r.start()
+        share.append((c, r))
+
+    def exchange(which, src_at, dst_at):
+        def copy(o):
+            peer = lax.rem(s + o, NSEQ)
+            return pltpu.make_async_remote_copy(
+                src_ref=src_at(peer),
+                dst_ref=dst_at(s),
+                send_sem=a_send.at[which, o],
+                recv_sem=a_recv.at[which, o],
+                device_id=(peer, b),
+                device_id_type=MESH_ID,
+            )
+
+        def begin(o, _):
+            copy(o).start()
+            return _
+
+        def finish(o, _):
+            copy(o).wait()
+            return _
+
+        def start():
+            lax.fori_loop(1, NSEQ, begin, 0)
+
+        def wait():
+            lax.fori_loop(1, NSEQ, finish, 0)
+
+        return start, wait
+
+    def lanes(i, size):
+        return pl.ds(pl.multiple_of(i * size, size), size)
+
+    n1 = n1_ref[...]
+    for k in range(8):
+        left[k] = flip(n1[:, k * BLOCK : (k + 1) * BLOCK])
+    share_group(0, left, left_hbm, 0, 8)
+    copies[0].wait()
+
+    def qkv_tile(t, _):
+        part = lanes(t, 512)
+        piece = (mm(n1, wqkv[:, part]) + bias_ref[:, part]).astype(BF)
+        which = t // 2
+        first = lax.rem(t, 2) * 8
+        for k in range(4):
+            turned = flip(piece[:, k * BLOCK : (k + 1) * BLOCK])
+            for half in range(2):
+                slab[first + 2 * k + half, pl.ds(which * HD, HD), :] = turned[
+                    half * HD : (half + 1) * HD
+                ]
+        return _
+
+    lax.fori_loop(0, 6, qkv_tile, 0)
+    start, wait = exchange(0, lambda p: slab.at[p], lambda p: qkv_t.at[:, lanes(p, TOK)])
+    start()
+    qkv_t[:, lanes(s, TOK)] = slab[s]
+    wait()
+
+    scale2 = LOG2E / math.sqrt(HD)
+
+    def to_rows(t, _):
+        part = lanes(t, TOK)
+        rows = pl.ds(pl.multiple_of(t * TOK, TOK), TOK)
+        q_row[rows, :] = flip(qkv_t[0:HD, part])
+        k_row[rows, :] = flip(qkv_t[HD : 2 * HD, part])
+        v_row[rows, :] = flip(qkv_t[2 * HD : 3 * HD, part])
+        return _
+
+    lax.fori_loop(0, NSEQ, to_rows, 0)
+    tiles = (NSEQ * TOK) // QCH
+
+    def forward_chunk(c, _):
+        part = lanes(c, QCH)
+        q_part = qkv_t[0:HD, part]
+        top = None
+        for t in range(tiles):
+            tile = slice(t * QCH, (t + 1) * QCH)
+            scores = mm(k_row[tile, :], q_part)
+            s_scr[tile, :] = scores
+            best = jnp.max(scores, 0, keepdims=True)
+            top = best if top is None else jnp.maximum(top, best)
+        top = top * scale2
+        total = jnp.zeros((1, QCH), F32)
+        mixed = jnp.zeros((HD, QCH), F32)
+        for t in range(tiles):
+            tile = slice(t * QCH, (t + 1) * QCH)
+            probs = jnp.exp2(s_scr[tile, :] * scale2 - top)
+            total = total + jnp.sum(probs, 0, keepdims=True)
+            mixed = mixed + mm(qkv_t[2 * HD : 3 * HD, tile], probs.astype(BF))
+        mixed = mixed / total
+        lse[c] = top + jnp.log2(total)
+        out_t32[:, part] = mixed
+        out_t[:, part] = mixed.astype(BF)
+        return _
+
+    lax.fori_loop(0, tiles, forward_chunk, 0)
+    start, wait = exchange(1, lambda p: out_t.at[:, lanes(p, TOK)], lambda p: o_in.at[p])
+    start()
+    o_in[s] = out_t[:, lanes(s, TOK)]
+    copies[1].wait()
+    wait()
+
+    parts = []
+    for k in range(8):
+        pair = jnp.concatenate([o_in[2 * k], o_in[2 * k + 1]], 0)
+        left[8 + k] = pair
+        parts.append(flip(pair))
+    share_group(1, left, left_hbm, 8, 8)
+    o_low = jnp.concatenate(parts, 1)
+    mid = h0_ref[...] + (mm(o_low, wo[...]) + vec_ref[7:8, :])
+    mid_s[...] = mid
+    unit, _ = normalise(mid)
+    n2 = (unit * vec_ref[3:4, :] + vec_ref[4:5, :]).astype(BF)
+    for k in range(8):
+        left[16 + k] = flip(n2[:, k * BLOCK : (k + 1) * BLOCK])
+    share_group(2, left, left_hbm, 16, 8)
+    copies[2].wait()
+    copies[3].wait()
+    acc[...] = mid + vec_ref[8:9, :]
+
+    def up_tile(t, _):
+        part = lanes(t, 512)
+        upper = mm(n2, wup[:, part]) + bup_ref[:, part]
+        up_s[:, part] = upper
+        active = gelu_value(upper).astype(BF)
+        for k in range(4):
+            left[24 + 4 * t + k] = flip(active[:, k * BLOCK : (k + 1) * BLOCK])
+        acc[...] += mm(active, wdown[part, :])
+        return _
+
+    lax.fori_loop(0, 8, up_tile, 0)
+    share_group(3, left, left_hbm, 24, 32)
+
+    unit_f, rstd_f = normalise(acc[...])
+    final = (unit_f * vec_ref[5:6, :] + vec_ref[6:7, :]).astype(BF)
+    head = head_ref[...]
+    diff = mm(final, head) - goal_ref[...].astype(F32)
+    wave[0] = diff[0:64] + diff[64:128]
+    partners = (
+        sibling,
+        s + 2 - 4 * xpos,
+        s + 4 - 8 * lax.rem(zpos, 2),
+        s + 8 - 16 * (zpos // 2),
+    )
+    for k, partner in enumerate(partners):
+        r = pltpu.make_async_remote_copy(
+            src_ref=wave.at[2 * k],
+            dst_ref=wave.at[2 * k + 1],
+            send_sem=x_send.at[k],
+            recv_sem=x_recv.at[k],
+            device_id=(partner, b),
+            device_id_type=MESH_ID,
+        )
+        r.start()
+        r.wait()
+        wave[2 * k + 2] = wave[2 * k] + wave[2 * k + 1]
+    total_wave = wave[8]
+    one = lax.broadcasted_iota(jnp.int32, (HOUT, HOUT), 0)
+    two = lax.broadcasted_iota(jnp.int32, (HOUT, HOUT), 1)
+    swap = (one == two + 1 - 2 * (two % 2)).astype(F32)
+    other = mmh(total_wave, swap)
+    weight = wlat_ref[...]
+    square = jnp.sum(weight * diff * diff, keepdims=True)
+    cross = jnp.sum(weight[0:64] * total_wave * other, keepdims=True) * (1.0 / NSEQ)
+    loss_ref[...] = jnp.broadcast_to(
+        square * (1.0 / MSE_COUNT)
+        + (SPECTRAL / DFT_COUNT) * (float(KMODES) * square + cross),
+        loss_ref.shape,
+    )
+    other2 = jnp.concatenate([other, other], 0)
+    d_pred = weight * (
+        (2.0 / MSE_COUNT) * diff + (2.0 * SPECTRAL / DFT_COUNT) * (float(KMODES) * diff + other2)
+    )
+    d_low = d_pred.astype(BF)
+    ghead_ref[...] = mm(final, d_low, TN)
+    d_final = mm(d_low, head, NT)
+    gvec_ref[5:6, :] = column_sum(d_final * unit_f)
+    gvec_ref[6:7, :] = column_sum(d_final)
+    d_out = normalise_back(d_final, unit_f, rstd_f, vec_ref[5:6, :])
+    d_branch = d_out.astype(BF)
+    gvec_ref[8:9, :] = column_sum(d_branch.astype(F32))
+    for k in range(8):
+        right[64 + k] = d_branch[:, k * BLOCK : (k + 1) * BLOCK]
+    share_group(4, right, right_hbm, 64, 8)
+    acc[...] = jnp.zeros_like(acc)
+
+    def down_tile(t, _):
+        part = lanes(t, 512)
+        d_active = mm(d_branch, wdown[part, :], NT)
+        d_upper = (d_active * gelu_slope(up_s[:, part])).astype(BF)
+        gup_ref[:, part] = column_sum(d_upper.astype(F32))
+        for k in range(4):
+            right[32 + 4 * t + k] = d_upper[:, k * BLOCK : (k + 1) * BLOCK]
+        acc[...] += mm(d_upper, wup[:, part], NT)
+        return _
+
+    lax.fori_loop(0, 8, down_tile, 0)
+    share_group(5, right, right_hbm, 32, 32)
+    d_n2 = acc[...]
+    unit, rstd = normalise(mid_s[...])
+    gvec_ref[3:4, :] = column_sum(d_n2 * unit)
+    gvec_ref[4:5, :] = column_sum(d_n2)
+    d_mid = d_out + normalise_back(d_n2, unit, rstd, vec_ref[3:4, :])
+    mid_s[...] = d_mid
+    d_mid_low = d_mid.astype(BF)
+    gvec_ref[7:8, :] = column_sum(d_mid_low.astype(F32))
+    for k in range(8):
+        right[24 + k] = d_mid_low[:, k * BLOCK : (k + 1) * BLOCK]
+    share_group(6, right, right_hbm, 24, 8)
+    d_att = mm(d_mid_low, wo[...], NT).astype(BF)
+    for k in range(8):
+        turned = flip(d_att[:, k * BLOCK : (k + 1) * BLOCK])
+        d_slab[2 * k] = turned[0:HD]
+        d_slab[2 * k + 1] = turned[HD : 2 * HD]
+    start, wait = exchange(2, lambda p: d_slab.at[p], lambda p: do_t.at[:, lanes(p, TOK)])
+    start()
+    do_t[:, lanes(s, TOK)] = d_slab[s]
+    wait()
+
+    def do_rows(t, _):
+        rows = pl.ds(pl.multiple_of(t * TOK, TOK), TOK)
+        do_row[rows, :] = flip(do_t[:, lanes(t, TOK)])
+        return _
+
+    lax.fori_loop(0, NSEQ, do_rows, 0)
+    dk_acc[...] = jnp.zeros_like(dk_acc)
+    dv_acc[...] = jnp.zeros_like(dv_acc)
+    scale = 1.0 / math.sqrt(HD)
+
+    def backward_chunk(c, _):
+        part = lanes(c, QCH)
+        rows = pl.ds(pl.multiple_of(c * QCH, QCH), QCH)
+        q_part = qkv_t[0:HD, part]
+        do_part = do_t[:, part]
+        delta = jnp.sum(do_part.astype(F32) * out_t32[:, part], 0, keepdims=True)
+        base = lse[c]
+        q_rows = q_row[rows, :]
+        g_rows = do_row[rows, :]
+        d_query = jnp.zeros((HD, QCH), F32)
+        for t in range(tiles):
+            tile = slice(t * QCH, (t + 1) * QCH)
+            probs = jnp.exp2(mm(k_row[tile, :], q_part) * scale2 - base)
+            d_prob = mm(v_row[tile, :], do_part)
+            d_score = (probs * (d_prob - delta)).astype(BF)
+            dv_acc[tile, :] += mm(probs.astype(BF), g_rows)
+            dk_acc[tile, :] += mm(d_score, q_rows)
+            d_query = d_query + mm(qkv_t[HD : 2 * HD, tile], d_score)
+        dqkv_t[0:HD, part] = (d_query * scale).astype(BF)
+        return _
+
+    lax.fori_loop(0, tiles, backward_chunk, 0)
+
+    def turn_back(t, _):
+        part = lanes(t, TOK)
+        rows = pl.ds(pl.multiple_of(t * TOK, TOK), TOK)
+        dqkv_t[HD : 2 * HD, part] = flip((dk_acc[rows, :] * scale)).astype(BF)
+        dqkv_t[2 * HD : 3 * HD, part] = flip(dv_acc[rows, :]).astype(BF)
+        return _
+
+    lax.fori_loop(0, NSEQ, turn_back, 0)
+    start, wait = exchange(3, lambda p: dqkv_t.at[:, lanes(p, TOK)], lambda p: dqkv_in.at[p])
+    start()
+    dqkv_in[s] = dqkv_t[:, lanes(s, TOK)]
+    wait()
+
+    def place(j, _):
+        for which in range(3):
+            part = slice(which * HD, (which + 1) * HD)
+            pair = jnp.concatenate([dqkv_in[2 * j, part, :], dqkv_in[2 * j + 1, part, :]], 0)
+            right[8 * which + j] = flip(pair)
+        return _
+
+    lax.fori_loop(0, 8, place, 0)
+    share_group(7, right, right_hbm, 0, 24)
+    acc[...] = jnp.zeros_like(acc)
+
+    def in_tile(t, _):
+        piece = jnp.concatenate([right[4 * t + k] for k in range(4)], 1)
+        acc[...] += mm(piece, wqkv[:, lanes(t, 512)], NT)
+        return _
+
+    lax.fori_loop(0, 6, in_tile, 0)
+    for k in range(8):
+        part = slice(k * BLOCK, (k + 1) * BLOCK)
+        gvec_ref[9:10, part] = column_sum(right[k].astype(F32))
+        gvec_ref[10:11, part] = column_sum(right[16 + k].astype(F32))
+    d_n1 = acc[...]
+    unit, rstd = normalise(h0_ref[...])
+    gvec_ref[1:2, :] = column_sum(d_n1 * unit)
+    gvec_ref[2:3, :] = column_sum(d_n1)
+    drow_ref[...] = mid_s[...] + normalise_back(d_n1, unit, rstd, vec_ref[1:2, :])
+    gvec_ref[0:1, :] = jnp.zeros((1, D), F32)
+    gvec_ref[11:16, :] = jnp.zeros((5, D), F32)
+    for c, r in share:
+        c.wait()
+        r.wait()
+
+
+def run_layer(n1, h0, vec, bias, bup, goals, head_low, wlat, mats):
+    vmem = pl.BlockSpec(memory_space=VM)
+    anyspace = pl.BlockSpec(memory_space=pl.ANY)
+    length = NSEQ * TOK
+    return pl.pallas_call(
+        layer_kernel,
+        name="layer",
+        out_shape=(
+            jax.ShapeDtypeStruct((2, N_LEFT, BLOCK, TOK), BF),
+            jax.ShapeDtypeStruct((2, N_RIGHT, TOK, BLOCK), BF),
+            jax.ShapeDtypeStruct((TOK, D), F32),
+            jax.ShapeDtypeStruct((16, D), F32),
+            jax.ShapeDtypeStruct((1, FF), F32),
+            jax.ShapeDtypeStruct((D, HOUT), F32),
+            jax.ShapeDtypeStruct((8, 128), F32),
+        ),
+        in_specs=[vmem] * 8 + [anyspace] * 4,
+        out_specs=(anyspace, anyspace) + (vmem,) * 5,
+        scratch_shapes=[
+            VM((D, 3 * D), BF),
+            VM((D, D), BF),
+            VM((D, FF), BF),
+            VM((FF, D), BF),
+            VM((N_LEFT, BLOCK, TOK), BF),
+            VM((N_RIGHT, TOK, BLOCK), BF),
+            VM((HEADS, 3 * HD, TOK), BF),
+            VM((3 * HD, length), BF),
+            VM((HD, length), BF),
+            VM((HD, length), F32),
+            VM((length // QCH, 1, QCH), F32),
+            VM((HEADS, HD, TOK), BF),
+            VM((HEADS, HD, TOK), BF),
+            VM((HD, length), BF),
+            VM((3 * HD, length), BF),
+            VM((HEADS, 3 * HD, TOK), BF),
+            VM((length, HD), BF),
+            VM((length, HD), BF),
+            VM((length, HD), BF),
+            VM((length, HD), BF),
+            VM((length, QCH), F32),
+            VM((length, HD), F32),
+            VM((length, HD), F32),
+            VM((TOK, D), F32),
+            VM((TOK, FF), F32),
+            VM((TOK, D), F32),
+            VM((9, 64, HOUT), F32),
+            pltpu.SemaphoreType.DMA((4,)),
+            pltpu.SemaphoreType.DMA((4, NSEQ)),
+            pltpu.SemaphoreType.DMA((4, NSEQ)),
+            pltpu.SemaphoreType.DMA((4,)),
+            pltpu.SemaphoreType.DMA((4,)),
+            pltpu.SemaphoreType.DMA((8,)),
+            pltpu.SemaphoreType.DMA((8,)),
+            pltpu.SemaphoreType.DMA((8,)),
+        ],
+        compiler_params=pltpu.CompilerParams(
+            collective_id=1, has_side_effects=True, vmem_limit_bytes=60 * 1024 * 1024
+        ),
+    )(n1, h0, vec, bias, bup, goals, head_low, wlat, *mats)
+
+
+def token_maps():
+    row = lax.broadcasted_iota(jnp.int32, (VARS, HOUT), 0)
+    col = lax.broadcasted_iota(jnp.int32, (VARS, HOUT), 1)
+    return (col // 4 == row).astype(F32)
+
+
+def embed_kernel(pix_ref, ids_ref, lead_ref, emb_ref, vec_ref, h0_ref, n1_ref, xp_ref, a_ref):
+    slot = lax.broadcasted_iota(jnp.int32, (HOUT, HOUT), 1)
+    place = (ids_ref[...] == slot).astype(BF)
+    pix = mm(pix_ref[...], place)
+    xp_ref[...] = pix
+    tok = emb_ref[0:HOUT, :]
+    emb = emb_ref[HOUT : HOUT + VARS, :]
+    query = vec_ref[0:1, :]
+    spread = token_maps()
+    tok_q = jnp.sum(tok * query, -1, keepdims=True)
+    emb_q = mmh(query, emb, NT)
+    back = lax.broadcasted_iota(jnp.int32, (HOUT, VARS), 0) // 4
+    var = lax.broadcasted_iota(jnp.int32, (HOUT, VARS), 1)
+    reduce = jnp.where(back == var, tok_q, 0.0)
+    logits = (mmh(pix, reduce) + emb_q) * (1.0 / math.sqrt(D))
+    logits = logits - jnp.max(logits, -1, keepdims=True)
+    weights = jnp.exp(logits)
+    weights = weights / jnp.sum(weights, -1, keepdims=True)
+    a_ref[...] = weights
+    wide = mmh(weights, spread) * pix
+    lead = emb_ref[pl.ds(HOUT + VARS + lead_ref[0], 1), :]
+    h0 = mmh(wide, tok) + mmh(weights, emb) + lead
+    h0_ref[...] = h0
+    unit, _ = normalise(h0)
+    n1_ref[...] = (unit * vec_ref[1:2, :] + vec_ref[2:3, :]).astype(BF)
+
+
+def run_embed(pix, ids, lead, embed, vec):
+    vmem = pl.BlockSpec(memory_space=VM)
+    smem = pl.BlockSpec(memory_space=pltpu.SMEM)
+    return pl.pallas_call(
+        embed_kernel,
+        name="embed_fwd",
+        out_shape=(
+            jax.ShapeDtypeStruct((TOK, D), F32),
+            jax.ShapeDtypeStruct((TOK, D), BF),
+            jax.ShapeDtypeStruct((TOK, HOUT), F32),
+            jax.ShapeDtypeStruct((TOK, VARS), F32),
+        ),
+        in_specs=[vmem, vmem, smem, vmem, vmem],
+        out_specs=(vmem,) * 4,
+    )(pix, ids, lead, embed, vec)
+
+
+def embed_back_kernel(drow_ref, xp_ref, a_ref, lead_ref, emb_ref, vec_ref, gemb_ref, gq_ref):
+    d_rows = drow_ref[...]
+    pix = xp_ref[...]
+    weights = a_ref[...]
+    tok = emb_ref[0:HOUT, :]
+    emb = emb_ref[HOUT : HOUT + VARS, :]
+    query = vec_ref[0:1, :]
+    spread = token_maps()
+    d_wide = mmh(d_rows, tok, NT)
+    d_weight = mmh(pix * d_wide, spread, NT) + mmh(d_rows, emb, NT)
+    d_logit = (
+        weights
+        * (d_weight - jnp.sum(weights * d_weight, -1, keepdims=True))
+        * (1.0 / math.sqrt(D))
+    )
+    wide = mmh(weights, spread) * pix
+    d_wide_l = mmh(d_logit, spread) * pix
+    ones = jnp.ones((TOK, 1), F32)
+    d_tok_q = mmh(d_wide_l, ones, TN)
+    d_emb_q = mmh(d_logit, ones, TN)
+    gemb_ref[0:HOUT, :] = mmh(wide, d_rows, TN) + d_tok_q * query
+    gemb_ref[HOUT : HOUT + VARS, :] = mmh(weights, d_rows, TN) + d_emb_q * query
+    row = lax.broadcasted_iota(jnp.int32, (LEADS, D), 0)
+    gemb_ref[HOUT + VARS :, :] = jnp.where(row == lead_ref[0], column_sum(d_rows), 0.0)
+    gq_ref[...] = column_sum(d_tok_q * tok) + column_sum(d_emb_q * emb)
+
+
+def run_embed_back(d_rows, pix, weights, lead, embed, vec):
+    vmem = pl.BlockSpec(memory_space=VM)
+    smem = pl.BlockSpec(memory_space=pltpu.SMEM)
+    return pl.pallas_call(
+        embed_back_kernel,
+        name="embed_bwd",
+        out_shape=(
+            jax.ShapeDtypeStruct((EROWS, D), F32),
+            jax.ShapeDtypeStruct((1, D), F32),
+        ),
+        in_specs=[vmem, vmem, vmem, smem, vmem, vmem],
+        out_specs=(vmem,) * 2,
+    )(d_rows, pix, weights, lead, embed, vec)
+
+
+def fast_shards(
+    inputs,
+    targets,
+    var_ids,
+    lead_ids,
+    block_order,
+    blocks,
+    block_momentum,
+    left_stats,
+    right_stats,
+    left_roots,
+    right_roots,
+    embed_params,
+    embed_first,
+    embed_second,
+    vectors,
+    vector_first,
+    vector_second,
+    head_weight,
+    head_first,
+    head_second,
+):
+    stack = lax.all_gather(blocks.astype(BF), ("seq", "batch"), axis=0, tiled=True)
+    natural = jnp.zeros_like(stack).at[block_order].set(stack)
+    mats = split_matrices(natural)
+    ids = (4 * var_ids[0][:, None] + jnp.arange(4, dtype=jnp.int32)[None]).reshape(HOUT, 1)
+    h0, n1, pix, weights = run_embed(inputs[0], ids, lead_ids, embed_params, vectors)
+    bias = jnp.concatenate([vectors[9], jnp.zeros_like(vectors[9]), vectors[10]])[None]
+    bup = vectors[11:].reshape(1, FF)
+    nlat = 2 * LAT_P
+    lat = ((jnp.arange(nlat, dtype=jnp.float32) + 0.5) / nlat - 0.5) * math.pi
+    wlat = jnp.cos(lat)
+    wlat = wlat / jnp.mean(wlat)
+    wlat = jnp.broadcast_to(
+        wlat.reshape(1, LAT_P, 1, 2, 1), (TOK // LAT_P, LAT_P, VARS, 2, 2)
+    ).reshape(TOK, HOUT)
+    left, right, d_rows, g_vec, g_up, g_head, loss = run_layer(
+        n1, h0, vectors, bias, bup, targets[0], head_weight.astype(BF), wlat, mats
+    )
+    g_embed, g_query = run_embed_back(d_rows, pix, weights, lead_ids, embed_params, vectors)
+    g_vectors = jnp.concatenate([g_query, g_vec[1:11], g_up.reshape(-1, D)])
+    pairs = ((0, 8, 0, 24), (8, 16, 24, 32), (16, 24, 32, 64), (24, 56, 64, 72))
+    grads = jnp.concatenate(
+        [
+            jnp.einsum(
+                "rit,ctj->rcij", left[0, a:e], right[0, f:g], preferred_element_type=F32
+            ).reshape(-1, BLOCK, BLOCK)
+            for a, e, f, g in pairs
+        ]
+    )
+    owned = lax.psum_scatter(
+        grads[block_order], ("seq", "batch"), scatter_dimension=0, tiled=True
+    )
+    g_embed, g_vectors, g_head, loss_total = lax.psum(
+        (g_embed, g_vectors, g_head, loss[0, 0]), ("seq", "batch")
+    )
+    rest_squares = (
+        jnp.sum(g_embed * g_embed) + jnp.sum(g_vectors * g_vectors) + jnp.sum(g_head * g_head)
+    )
+    grad_norm = jnp.sqrt(lax.psum(jnp.sum(owned * owned), ("seq", "batch")) + rest_squares)
+    clip = CLIP_NORM / jnp.maximum(grad_norm, CLIP_NORM)
+    owned = owned * clip
+    new_momentum = BETA_ONE * block_momentum + (1.0 - BETA_ONE) * owned
+    new_left = BETA_TWO * left_stats + (1.0 - BETA_TWO) * jnp.einsum(
+        "bij,bkj->bik", owned, owned, precision=HIGH
+    )
+    new_right = BETA_TWO * right_stats + (1.0 - BETA_TWO) * jnp.einsum(
+        "bji,bjk->bik", owned, owned, precision=HIGH
+    )
+    direction = jnp.einsum(
+        "bij,bjk->bik",
+        jnp.einsum("bij,bjk->bik", left_roots, new_momentum, precision=HIGH),
+        right_roots,
+        precision=HIGH,
+    )
+    new_blocks = blocks - SHAMPOO_RATE * (direction + DECAY * blocks)
+    e_one, e_two, e_new = adam(embed_params, embed_first, embed_second, g_embed * clip, EMBED_RATE)
+    v_one, v_two, v_new = adam(vectors, vector_first, vector_second, g_vectors * clip, VECTOR_RATE)
+    h_one, h_two, h_new = adam(head_weight, head_first, head_second, g_head * clip, HEAD_RATE)
+    return (
+        loss_total,
+        grad_norm,
+        new_blocks,
+        new_momentum,
+        new_left,
+        new_right,
+        e_one,
+        e_two,
+        e_new,
+        v_one,
+        v_two,
+        v_new,
+        h_one,
+        h_two,
+        h_new,
+    )
+
+
 def solution(mesh):
     in_specs = (
         P("batch", "seq", None),
@@ -483,4 +1193,6 @@
         P(),
         P(),
     )
-    return jax.shard_map(shards, mesh=mesh, in_specs=in_specs, out_specs=out_specs, check_vma=False)
+    sizes = dict(mesh.shape)
+    fast = sizes == {"seq": NSEQ, "batch": 2}
+    return jax.shard_map(fast_shards if fast else shards, mesh=mesh, in_specs=in_specs, out_specs=out_specs, check_vma=False)

time: 1770 us -> 1250 us (0.71)
  matrix products: 409 us -> 43.1 us
  Pallas kernels: 0 us -> 127 us
  local copies, waits for them, and re-layouts: 416 us -> 321 us
  loops' own time: 94.8 us -> 0 us
  other arithmetic: 102 us -> 56 us
  blocking collectives: 79.1 us -> 40 us
    dot_general x144 -> x8, matrix products: 409 us -> 43.1 us  [the longest x4 30 us: fast_shards(): jnp.einsum('rit,ctj->rcij', left[0, a:e], right[0, f:g], preferred_elemen...]
    pallas_call x0 -> x3, Pallas kernels: none -> 127 us  [the longest x1 117 us: run_layer(): pl.pallas_call(layer_kernel, name='layer', out_shape=(jax.ShapeDtypeStruc...]
    reshape x15 -> x3, local copies, waits for them, and re-layouts: 111 us -> 0.93 us  [the longest x2 0.91 us: fast_shards(): wlat = jnp.broadcast_to(wlat.reshape(1, LAT_P, 1, 2, 1), (TOK // LAT_P, L...]
    another operation x3 -> x0, loops' own time: 94.8 us -> none  [the longest x1 32 us: attention_forward(): inner, _ = lax.scan(visit, start_state, jnp.arange(count))]
    transpose x0 -> x8, local copies, waits for them, and re-layouts: none -> 94.3 us  [the longest x4 53.1 us: fast_shards(): jnp.einsum('rit,ctj->rcij', left[0, a:e], right[0, f:g], preferred_elemen...]
    dynamic_slice x80 -> x0, local copies, waits for them, and re-layouts: 55.4 us -> none  [the longest x48 28.1 us: attention_forward(): inner, _ = lax.scan(visit, start_state, jnp.arange(count))]
    all_gather x2 -> x0, blocking collectives: 39.2 us -> none  [the longest x1 19.8 us: attention_backward(): lax.all_gather(delta, 'seq', axis=1, tiled=True)]
    reduce_sum x38 -> x5, other arithmetic: 26 us -> 7.92 us  [the longest x1 2.42 us: fast_shards(): jnp.sum(owned * owned)]
  transfers between devices with their start and end apart: 8 -> 3, of which waited for: 5 -> 3; matrix products, arithmetic and copies ran while one was open for 27% -> 7% of each run, Pallas kernels for 0% -> 0%
where the time goes in v1:
time: 1250 us
  waiting for transfers between devices  641 us (51%)
  local copies, waits for them, and re-layouts  321 us (26%)
  Pallas kernels  127 us (10%)
  other arithmetic  56 us (4%)
  matrix products  43.1 us (3%)
  blocking collectives  40 us (3%)
  between operations  19.7 us (2%)
    reduce_scatter x1, waiting for transfers between devices, fast_shards(): lax.psum_scatter(grads[block_order], ('seq', 'batch'), scatter_dimension=...  434 us
    all_gather x1, waiting for transfers between devices, fast_shards(): lax.all_gather(blocks.astype(BF), ('seq', 'batch'), axis=0, tiled=True)  145 us
    pallas_call x1, Pallas kernels, run_layer(): pl.pallas_call(layer_kernel, name='layer', out_shape=(jax.ShapeDtypeStruc...  117 us
    scatter x1, local copies, waits for them, and re-layouts, fast_shards(): natural = jnp.zeros_like(stack).at[block_order].set(stack)  112 us
    psum x1, waiting for transfers between devices, fast_shards(): lax.psum((g_embed, g_vectors, g_head, loss[0, 0]), ('seq', 'batch'))  61.5 us
    transpose x4, local copies, waits for them, and re-layouts, fast_shards(): jnp.einsum('rit,ctj->rcij', left[0, a:e], right[0, f:g], preferred_elemen...  53.1 us
    unnamed x64, local copies, waits for them, and re-layouts  46.9 us
    transpose x4, local copies, waits for them, and re-layouts, from_blocks(): return stack.reshape(rows // size, cols // size, size, size).transpose(0,...  41.2 us
  transfers between devices with their start and end apart: 3, of which 3 were waited for; matrix products, arithmetic and copies ran while one was open for 7% of the time, Pallas kernels for 0%

profile of v1, /device:TPU:0, one launch (start us, length us, event | category | flops | bytes accessed | tf_op | source)
XLA Modules:
  0.0 1247.5 jit_solution(2617920990666238974)
XLA Ops:
  23.9 145.1 %all-gather.2.cloned.1.call-done = bf16[768,128,128]{2,1,0:T(8,128)(2,1)} async-done(((bf16[24,128,128]{2,1,0:T(8,128)(2,1)}), bf16[768,128,128]{2,1,0:T(8,128)(2,1)}) %all-gather.2.cloned.1.call-update) | async-done | bytes 25165840 | tf_op jit(solution)/shard_map/all_gather | solution.py:1080
  169.0 8.9 broadcast_in_dim.22
  177.9 112.1 %scatter_fusion = bf16[768,128,128]{2,1,0:T(8,128)(2,1)} fusion(bf16[768,128,128]{2,1,0:T(8,128)(2,1)} %broadcast_in_dim.22, s32[768]{0:T(1024)S(1)} %compare_select_fusion, bf16[768,128,128]{2,1,0:T(8,128)(2,1)} %all-gather.2.cloned.1.call-done), kind=kCustom, calls=%fused_computation.1 | custom fusion | bytes 75500544 | tf_op jit(solution)/shard_map/scatter | solution.py:1081
  295.8 12.3 fusion.26
  312.2 4.7 copy.156
  320.2 12.2 copy.107
  332.4 15.1 %copy.155 = bf16[128,8,32,128]{3,1,2,0:T(8,128)(2,1)} copy(bf16[128,8,32,128]{3,2,1,0:T(8,128)(2,1)} %bitcast.111) | data formatting | bytes 16777216
  347.5 23.6 %copy.108 = bf16[32,128,8,128]{3,2,1,0:T(8,128)(2,1)} copy(bf16[32,128,8,128]{3,1,2,0:T(8,128)(2,1)} %bitcast.113) | data formatting | bytes 16777216 | tf_op jit(solution)/shard_map/transpose | solution.py:59
  371.1 8.8 copy.154
  379.9 116.7 %layer.1 = (bf16[2,56,128,128]{3,2,1,0:T(8,128)(2,1)}, bf16[2,72,128,128]{3,2,1,0:T(8,128)(2,1)}, f32[128,1024]{1,0:T(8,128)}, f32[16,1024]{1,0:T(8,128)}, f32[1...) custom-call(bf16[128,1024]{1,0:T(8,128)(2,1)} %get-tuple-element.28.n1_ref, ...), custom_call_target="tpu_custom_call" | custom-call | tf_op jit(solution)/shard_map/layer/pallas_call | solution.py:909
  496.5 9.4 convolution_bitcast_fusion
  506.0 9.3 convolution_bitcast_fusion.1
  519.1 7.5 convolution_bitcast_fusion.2
  526.5 17.5 %copy.118 = f32[32,8,128,128]{3,2,1,0:T(8,128)} copy(f32[32,8,128,128]{2,3,0,1:T(8,128)} %convolution_bitcast_fusion) | data formatting | bytes 33554432 | tf_op jit(solution)/shard_map/rit,ctj->rcij/transpose | solution.py:1102
  544.0 17.5 %copy.116 = f32[8,32,128,128]{3,2,1,0:T(8,128)} copy(f32[8,32,128,128]{2,3,0,1:T(8,128)} %convolution_bitcast_fusion.1) | data formatting | bytes 33554432 | tf_op jit(solution)/shard_map/rit,ctj->rcij/transpose | solution.py:1102
  561.5 5.4 copy.114
  566.8 12.8 %copy.112 = f32[8,24,128,128]{3,2,1,0:T(8,128)} copy(f32[8,24,128,128]{2,3,0,1:T(8,128)} %convolution_bitcast_fusion.2) | data formatting | bytes 25165824 | tf_op jit(solution)/shard_map/rit,ctj->rcij/transpose | solution.py:1102
  579.7 5.8 embed_bwd.1
  585.5 34.6 %pad_maximum_fusion = f32[768,128,128]{2,1,0:T(8,128)} fusion(f32[256,128,128]{2,1,0:T(8,128)} %bitcast.106, f32[256,128,128]{2,1,0:T(8,128)} %bitcast.107, f32[64,128,128]{2,1,0:T(8,128)} %bitcast.118, f32[192,128,128]{2,1,0:T(8,128)} %bitcast.108), kind=kLoop, calls=%fused_computation.2 | loop fusion | flops 37748736 | bytes 100663296 | tf_op jit(solution)/shard_map/concatenate | solution.py:1100
  620.2 35.6 %gather_fusion = f32[768,128,128]{2,1,0:T(8,128)} fusion(f32[768,128,128]{2,1,0:T(8,128)} %pad_maximum_fusion, s32[1024]{0:T(1024)S(1)} %copy-done.20), kind=kCustom, calls=%fused_computation | custom fusion | bytes 100666368 | tf_op jit(solution)/shard_map/gather | solution.py:1109
  663.6 61.5 %all-reduce.4.cloned.1.call-done = (f32[272,1024]{1,0:T(8,128)}, f32[1024,192]{1,0:T(8,128)}) async-done(((f32[272,1024]{1,0:T(8,128)}, f32[1024,192]{1,0:T(8,128)}), (f32[272,1024]{1,0:T(8,128)}, f32[1024,192]{1,0:T(8,128)})) %all-reduce.4.cloned.1.call-update) | async-done | bytes 1900560 | tf_op jit(solution)/shard_map/psum | solution.py:1111
  729.3 434.1 %reduce-scatter.2.cloned.1.call-done = f32[24,128,128]{2,1,0:T(8,128)} async-done(((f32[768,128,128]{2,1,0:T(8,128)}), f32[24,128,128]{2,1,0:T(8,128)}) %reduce-scatter.2.cloned.1.call-update) | async-done | bytes 1572880 | tf_op jit(solution)/shard_map/reduce_scatter | solution.py:1108
  1165.8 40.0 %all-reduce = (f32[]{:T(128)}, f32[]{:T(128)}, f32[15,1024]{1,0:T(8,128)S(1)}) all-reduce(f32[]{:T(128)} %bitcast.14, f32[]{:T(128)} %multiply_reduce_fusion, f32[15,1024]{1,0:T(8,128)S(1)} %pad_maximum_fusion.1), channel_id=1, replica_groups=mesh['seq'=16,'batch'=2] {'seq','batch'}, use_global_device_ids=true, to_apply=%region_2.0 | all-reduce | flops 15362 | bytes 122896 | tf_op jit(solution)/shard_map/psum | solution.py:1111
  1231.0 4.5 multiply_add_fusion.1
  (106 shorter events, 73.1 us)
Async XLA Ops:
  7.2 1215.1 %copy-start = (f32[24,128,128]{2,1,0:T(8,128)S(1)}, f32[24,128,128]{2,1,0:T(8,128)}, u32[]{:S(2)}) copy-start(f32[24,128,128]{2,1,0:T(8,128)} %param.29) | copy-start | bytes 4718596
  7.2 2.7 copy-start.18
  7.2 3.5 copy-start.24
  7.2 6.3 copy-start.19
  7.2 7.1 copy-start.6
  7.2 161.7 %all-gather.2.cloned.1.call-start = ((), (), s32[]{:S(2)}) async-start(), calls=%async_computation.1 | async-start | bytes 25952256 | tf_op jit(solution)/shard_map/all_gather | solution.py:1080
  9.9 715.2 %all-reduce.4.cloned.1.call-start = ((), (), s32[]{:S(2)}) async-start(), calls=%async_computation.3 | async-start | bytes 4325376 | tf_op jit(solution)/shard_map/psum | solution.py:1111
  14.3 7.5 copy-start.23
  585.5 577.9 %reduce-scatter.2.cloned.1.call-start = ((), (), s32[]{:S(2)}) async-start(), calls=%async_computation.2 | async-start | bytes 51904512 | tf_op jit(solution)/shard_map/reduce_scatter | solution.py:1108
  585.5 34.7 %copy-start.20 = (s32[1024]{0:T(1024)S(1)}, s32[1024]{0:T(1024)}, u32[]{:S(2)}) copy-start(s32[1024]{0:T(1024)} %pad_clamp_fusion) | copy-start | bytes 12292
  657.3 2.6 copy-start.14
  657.3 5.6 copy-start.21
  657.3 6.3 copy-start.15
  657.3 6.3 copy-start.22
  1215.6 5.0 copy-start.1
  1222.3 2.4 copy-start.10
  1224.7 3.1 copy-start.2
  1224.7 3.1 copy-start.5
  1224.7 3.1 copy-start.12
  1224.7 3.1 copy-start.13
  1227.9 2.4 copy-start.11
  1227.9 2.4 copy-start.16
  1227.9 3.1 copy-start.8
  1231.0 4.5 copy-start.9
  (4 other events, 7.2 us)
Sparse Core Ops, SparseCore 0:
  11.5 157.3 all-gather.1
  585.6 139.4 all-reduce.3
  732.6 430.7 reduce-scatter.1

commit v2 on v1

--- a/solution.py
+++ b/solution.py
@@ -447,6 +447,281 @@
         h_two,
         h_new,
     )
+
+
+SHARE = 24
+PIECE = 6
+MAIN = ("zxy", "zyx", "xzy", "yzx")
+SMALL = ("xyz", "yxz")
+TAIL = ("xzy", "yzx")
+GATHER_ORDER = (
+    (0, 0, 0, 3), (3, 0, 0, 3), (1, 0, 0, 3), (2, 0, 0, 3), (0, 1, 0, 3), (1, 0, 0, 2), (0, 0, 0, 2), (1, 0, 0, 1),
+    (1, 0, 1, 3), (0, 0, 0, 1), (3, 0, 0, 2), (0, 0, 1, 3), (3, 0, 1, 3), (2, 1, 0, 3), (1, 1, 0, 3), (2, 0, 0, 2),
+    (1, 1, 1, 3), (0, 0, 0, 0), (1, 1, 0, 2), (2, 0, 1, 3), (1, 0, 1, 2), (2, 1, 0, 2), (3, 0, 1, 2), (0, 1, 0, 2),
+    (2, 0, 0, 1), (3, 1, 0, 3), (2, 0, 0, 0), (0, 0, 1, 2), (0, 1, 1, 3), (2, 0, 1, 2), (3, 0, 0, 1), (3, 1, 1, 3),
+    (0, 1, 0, 1), (2, 1, 1, 3), (3, 1, 0, 2), (1, 1, 0, 1), (2, 1, 0, 0), (1, 0, 0, 0), (3, 0, 0, 0), (1, 0, 1, 1),
+    (0, 1, 1, 2), (0, 0, 1, 1), (3, 0, 1, 0), (2, 1, 1, 2), (2, 1, 0, 1), (0, 1, 1, 1), (3, 1, 0, 1), (2, 0, 1, 1),
+    (0, 1, 0, 0), (3, 0, 1, 1), (1, 1, 1, 2), (1, 0, 1, 0), (3, 1, 0, 0), (1, 1, 0, 0), (0, 0, 1, 0), (3, 1, 1, 1),
+    (3, 1, 1, 0), (1, 1, 1, 0), (2, 1, 1, 1), (2, 1, 1, 0), (1, 1, 1, 1), (3, 1, 1, 2), (2, 0, 1, 0), (0, 1, 1, 0),
+)
+REDUCE_ORDER = (
+    (5, 0, 1, 0), (4, 0, 1, 0), (3, 1, 1, 1), (2, 1, 1, 0), (4, 1, 0, 0), (4, 0, 0, 0), (5, 0, 0, 0), (3, 1, 1, 0),
+    (3, 1, 0, 0), (2, 1, 1, 1), (5, 1, 1, 0), (4, 1, 0, 1), (1, 1, 1, 1), (4, 1, 1, 0), (4, 1, 1, 1), (4, 0, 1, 2),
+    (5, 1, 0, 1), (5, 1, 1, 2), (2, 0, 1, 0), (0, 1, 1, 0), (0, 0, 1, 0), (4, 0, 0, 2), (1, 1, 1, 0), (1, 1, 1, 3),
+    (5, 0, 1, 2), (5, 1, 0, 0), (5, 1, 1, 1), (0, 0, 1, 1), (1, 1, 0, 1), (5, 1, 0, 2), (2, 1, 0, 0), (2, 0, 1, 2),
+    (2, 1, 1, 2), (1, 1, 0, 2), (5, 1, 1, 3), (5, 0, 0, 1), (5, 0, 1, 1), (3, 0, 1, 0), (2, 0, 1, 1), (4, 0, 0, 1),
+    (5, 0, 0, 2), (4, 1, 0, 2), (3, 1, 0, 1), (3, 1, 0, 2), (3, 1, 0, 3), (0, 1, 1, 2), (4, 1, 1, 2), (0, 1, 1, 1),
+    (2, 1, 0, 1), (2, 0, 1, 3), (3, 1, 1, 2), (3, 0, 0, 0), (0, 1, 0, 0), (2, 0, 0, 0), (4, 0, 1, 1), (0, 1, 1, 3),
+    (3, 0, 1, 1), (2, 1, 0, 2), (2, 0, 0, 1), (1, 1, 1, 2), (1, 0, 1, 1), (3, 0, 0, 1), (1, 0, 1, 0), (2, 1, 1, 3),
+    (1, 1, 0, 0), (4, 0, 1, 3), (3, 0, 1, 2), (4, 1, 1, 3), (3, 1, 1, 3), (0, 1, 0, 1), (2, 0, 0, 2), (0, 0, 1, 2),
+    (3, 0, 0, 2), (1, 0, 1, 3), (5, 1, 0, 3), (1, 0, 0, 0), (0, 0, 1, 3), (0, 1, 0, 2), (1, 0, 1, 2), (0, 0, 0, 0),
+    (2, 1, 0, 3), (3, 0, 1, 3), (0, 0, 0, 1), (5, 0, 1, 3), (0, 1, 0, 3), (1, 0, 0, 1), (0, 0, 0, 2), (1, 1, 0, 3),
+    (4, 1, 0, 3), (1, 0, 0, 2), (0, 0, 0, 3), (3, 0, 0, 3), (5, 0, 0, 3), (2, 0, 0, 3), (4, 0, 0, 3), (1, 0, 0, 3),
+)
+TAIL_ORDER = (
+    (0, 0, 0, 3), (1, 0, 0, 3), (0, 0, 0, 2), (0, 1, 0, 3), (1, 0, 0, 2), (1, 0, 1, 3), (1, 1, 0, 3), (0, 0, 1, 3),
+    (0, 0, 0, 1), (0, 0, 0, 0), (0, 1, 0, 1), (0, 0, 1, 2), (1, 0, 0, 1), (0, 1, 0, 2), (0, 1, 1, 3), (1, 0, 1, 2),
+    (1, 0, 1, 1), (0, 0, 1, 1), (1, 1, 0, 2), (1, 0, 0, 0), (1, 1, 1, 3), (0, 1, 0, 0), (0, 1, 1, 1), (1, 1, 0, 1),
+    (1, 0, 1, 0), (1, 1, 0, 0), (0, 1, 1, 2), (1, 1, 1, 1), (1, 1, 1, 2), (0, 0, 1, 0), (1, 1, 1, 0), (0, 1, 1, 0),
+)
+
+
+class Place:
+    def __init__(self):
+        s = lax.axis_index("seq")
+        self.y = lax.axis_index("batch")
+        self.core = lax.rem(s, 2)
+        self.x = lax.rem(s // 2, 2)
+        self.z = s // 4
+        self.s = s
+
+    def chip(self, z, x, y):
+        return (z * 2 + x) * 2 + y
+
+    def linear(self, z, x, y):
+        return ((z * 2 + x) * 2 + self.core) * 2 + y
+
+    def device(self, z, x, y):
+        return ((z * 2 + x) * 2 + self.core, y)
+
+    def sibling(self):
+        return (self.s + 1 - 2 * self.core, self.y)
+
+    def far(self, rank):
+        z = self.z
+        if rank == 3:
+            return z
+        if rank == 2:
+            return z + 1 - 2 * lax.rem(z, 2)
+        low = z // 2
+        return (3 - 3 * low) if rank == 0 else (2 - low)
+
+    def flipped(self, dx, dy):
+        x = self.x if dx == 0 else 1 - self.x
+        y = self.y if dy == 0 else 1 - self.y
+        return x, y
+
+    def greet(self):
+        barrier = pltpu.get_barrier_semaphore()
+
+        def hail(device):
+            pl.semaphore_signal(barrier, inc=1, device_id=device, device_id_type=MESH_ID)
+
+        hail(self.sibling())
+        hail(self.device(self.z, 1 - self.x, self.y))
+        hail(self.device(self.z, self.x, 1 - self.y))
+
+        @pl.when(self.z < 3)
+        def _():
+            hail(self.device(self.z + 1, self.x, self.y))
+
+        @pl.when(self.z > 0)
+        def _():
+            hail(self.device(self.z - 1, self.x, self.y))
+
+        ends = (self.z == 0).astype(jnp.int32) + (self.z == 3).astype(jnp.int32)
+        pl.semaphore_wait(barrier, 5 - ends)
+
+
+def last_move(order, dx, dy, rank):
+    found = -1
+    for i, c in enumerate(order):
+        if (c == "x" and dx) or (c == "y" and dy) or (c == "z" and rank != 3):
+            found = i
+    return found
+
+
+def sends_before(order, axis):
+    count = 1
+    for c in order:
+        if c == axis:
+            return count
+        count *= 4 if c == "z" else 2
+    return count
+
+
+def drain(place, orders, total, sem, hops):
+    count = {c: sum(sends_before(order, c) for order in orders) for c in "xyz"}
+
+    def finish(i, pieces):
+        ref = total(pieces)
+        pltpu.make_async_remote_copy(
+            ref, ref, sem.at[i], sem.at[i], place.sibling(), MESH_ID
+        ).wait_send()
+
+    finish(0, count["x"])
+    finish(1, count["y"])
+    for z in range(4):
+        for i in (2, 3):
+            if hops[i - 2][z]:
+
+                @pl.when(place.z == z)
+                def _(i=i, z=z):
+                    finish(i, count["z"] * hops[i - 2][z])
+
+
+GATHER_HOPS = ((1, 2, 3, 0), (0, 3, 2, 1))
+REDUCE_HOPS = ((3, 2, 1, 0), (0, 1, 2, 3))
+
+
+def gather_tree(place, orders, steps, piece, total, recv, send, sib_send, sib_recv, between=None):
+    z = place.z
+    parts = len(orders)
+
+    def copy(ref, device, send_sem, recv_sem):
+        return pltpu.make_async_remote_copy(ref, ref, send_sem, recv_sem, device, MESH_ID)
+
+    for number, (part, dx, dy, rank) in enumerate(steps):
+        order = orders[part]
+        tz = place.far(rank)
+        sx, sy = place.flipped(dx, dy)
+        ref = piece(place.linear(tz, sx, sy) * parts + part)
+        landed = recv.at[part, place.chip(tz, sx, sy)]
+        own = dx == 0 and dy == 0 and rank == 3
+        if not own:
+            copy(ref, place.sibling(), landed, landed).wait_recv()
+        last = last_move(order, dx, dy, rank)
+        if last >= 0 and order[last] == "z" and rank != 3:
+            up = (z > tz).astype(jnp.int32)
+            nz = z + 2 * up - 1
+
+            @pl.when(jnp.logical_and(nz >= 0, nz <= 3))
+            def _():
+                copy(ref, place.device(nz, place.x, place.y), send.at[3 - up], landed).start()
+
+        for c in order[last + 1 :]:
+            if c == "x":
+                copy(ref, place.device(z, 1 - place.x, place.y), send.at[0], landed).start()
+            elif c == "y":
+                copy(ref, place.device(z, place.x, 1 - place.y), send.at[1], landed).start()
+            else:
+
+                @pl.when(z < 3)
+                def _():
+                    copy(ref, place.device(z + 1, place.x, place.y), send.at[2], landed).start()
+
+                @pl.when(z > 0)
+                def _():
+                    copy(ref, place.device(z - 1, place.x, place.y), send.at[3], landed).start()
+
+        copy(ref, place.sibling(), sib_send.at[0], sib_recv.at[0]).start()
+        if between is not None:
+            between(number)
+    drain(place, orders, total, send, GATHER_HOPS)
+    whole = total(16 * parts)
+    copy(whole, place.sibling(), sib_send.at[0], sib_recv.at[0]).wait()
+
+
+def radix(order, stop, dx, dy, tz):
+    index = 0
+    size = 1
+    for c in order[: order.index(stop)]:
+        value, base = {"x": (dx, 2), "y": (dy, 2), "z": (tz, 4)}[c]
+        index = index * base + value
+        size *= base
+    if stop == "z":
+        index = index * 4 + tz
+        size *= 4
+    return index, size
+
+
+def landing_base(orders):
+    base = {}
+    at = 0
+    for axis in ("x", "y", "z+", "z-"):
+        for part, order in enumerate(orders):
+            base[(axis, part)] = at
+            at += radix(order, axis[0], 0, 0, 0)[1]
+    return base, at
+
+
+def reduce_step(place, orders, base, step, own_piece, add_landed, land, recv, out, send, keep, offset):
+    part, dx, dy, rank = step
+    order = orders[part]
+    z = place.z
+    tz = place.far(rank)
+    tx, ty = place.flipped(dx, dy)
+    chip = place.chip(tz, tx, ty)
+    root = dx == 0 and dy == 0 and rank == 3
+    last = last_move(order, dx, dy, rank)
+    out_at = part * 16 + chip
+    own_piece(part + offset, place.linear(tz, tx, ty), chip, out_at)
+
+    def slot(axis):
+        return base[(axis, part)] + radix(order, axis[0], dx, dy, tz)[0]
+
+    def take(index):
+        ref = land.at[index]
+        sem = recv.at[index]
+        pltpu.make_async_remote_copy(ref, ref, sem, sem, place.sibling(), MESH_ID).wait_recv()
+        add_landed(part + offset, index)
+
+    if last >= 0 and order[last] == "z" and rank != 3:
+        up = (z > tz).astype(jnp.int32)
+        nz = z + 2 * up - 1
+        plus = base[("z+", part)]
+        minus = base[("z-", part)]
+        here = radix(order, "z", dx, dy, tz)[0]
+
+        @pl.when(jnp.logical_and(nz >= 0, nz <= 3))
+        def _():
+            take(up * plus + (1 - up) * minus + here)
+
+    for c in order[last + 1 :]:
+        if c == "z":
+
+            @pl.when(z < 3)
+            def _():
+                take(slot("z+"))
+
+            @pl.when(z > 0)
+            def _():
+                take(slot("z-"))
+
+        else:
+            take(slot(c))
+    keep(part + offset, out_at, root)
+    if root:
+        return
+    ref = out.at[out_at]
+
+    def push(device, index, direction):
+        pltpu.make_async_remote_copy(
+            ref, land.at[index], send.at[direction], recv.at[index], device, MESH_ID
+        ).start()
+
+    axis = order[last]
+    if axis == "x":
+        index = base[("x", part)] + radix(order, "x", 0, dy, tz)[0]
+        push(place.device(z, 1 - place.x, place.y), index, 0)
+    elif axis == "y":
+        index = base[("y", part)] + radix(order, "y", dx, 0, tz)[0]
+        push(place.device(z, place.x, 1 - place.y), index, 1)
+    else:
+        down = (z > tz).astype(jnp.int32)
+        here = radix(order, "z", dx, dy, tz)[0]
+        index = down * base[("z+", part)] + (1 - down) * base[("z-", part)] + here
+        push(place.device(z + 1 - 2 * down, place.x, place.y), index, 2 + down)
 
 
 TOK = 128
@@ -996,24 +1271,9 @@
     n1_ref[...] = (unit * vec_ref[1:2, :] + vec_ref[2:3, :]).astype(BF)
 
 
-def run_embed(pix, ids, lead, embed, vec):
-    vmem = pl.BlockSpec(memory_space=VM)
-    smem = pl.BlockSpec(memory_space=pltpu.SMEM)
-    return pl.pallas_call(
-        embed_kernel,
-        name="embed_fwd",
-        out_shape=(
-            jax.ShapeDtypeStruct((TOK, D), F32),
-            jax.ShapeDtypeStruct((TOK, D), BF),
-            jax.ShapeDtypeStruct((TOK, HOUT), F32),
-            jax.ShapeDtypeStruct((TOK, VARS), F32),
-        ),
-        in_specs=[vmem, vmem, smem, vmem, vmem],
-        out_specs=(vmem,) * 4,
-    )(pix, ids, lead, embed, vec)
-
-
-def embed_back_kernel(drow_ref, xp_ref, a_ref, lead_ref, emb_ref, vec_ref, gemb_ref, gq_ref):
+def embed_back_kernel(
+    drow_ref, xp_ref, a_ref, lead_ref, emb_ref, vec_ref, gvec_ref, gup_ref, ghead_ref, loss_ref, small_ref
+):
     d_rows = drow_ref[...]
     pix = xp_ref[...]
     weights = a_ref[...]
@@ -1033,26 +1293,390 @@
     ones = jnp.ones((TOK, 1), F32)
     d_tok_q = mmh(d_wide_l, ones, TN)
     d_emb_q = mmh(d_logit, ones, TN)
-    gemb_ref[0:HOUT, :] = mmh(wide, d_rows, TN) + d_tok_q * query
-    gemb_ref[HOUT : HOUT + VARS, :] = mmh(weights, d_rows, TN) + d_emb_q * query
+    g_tok = mmh(wide, d_rows, TN) + d_tok_q * query
+    g_emb = mmh(weights, d_rows, TN) + d_emb_q * query
     row = lax.broadcasted_iota(jnp.int32, (LEADS, D), 0)
-    gemb_ref[HOUT + VARS :, :] = jnp.where(row == lead_ref[0], column_sum(d_rows), 0.0)
-    gq_ref[...] = column_sum(d_tok_q * tok) + column_sum(d_emb_q * emb)
-
-
-def run_embed_back(d_rows, pix, weights, lead, embed, vec):
+    g_lead = jnp.where(row == lead_ref[0], column_sum(d_rows), 0.0)
+    g_query = column_sum(d_tok_q * tok) + column_sum(d_emb_q * emb)
+
+    def put(begin, value):
+        rows = value.shape[0]
+        at = 0
+        while at < rows:
+            device, inside = divmod(begin + at, ROWS)
+            count = min(rows - at, ROWS - inside)
+            small_ref[device, inside : inside + count, :] = value[at : at + count]
+            at += count
+
+    for k in range(8):
+        part = slice(k * BLOCK, (k + 1) * BLOCK)
+        put(EROWS * k, g_tok[:, part])
+        put(EROWS * k + HOUT, g_emb[:, part])
+        put(EROWS * k + HOUT + VARS, g_lead[:, part])
+        rows = [g_query[:, part], gvec_ref[1:11, part]]
+        rows += [gup_ref[:, r * D + k * BLOCK : r * D + (k + 1) * BLOCK] for r in range(4)]
+        put(VEC_AT + 16 * k, jnp.concatenate(rows + [jnp.zeros((1, BLOCK), F32)], 0))
+    put(HEAD_AT, ghead_ref[:, 0:BLOCK])
+    rest = jnp.concatenate(
+        [ghead_ref[:, BLOCK:HOUT], jnp.zeros((D, 2 * BLOCK - HOUT), F32)], 1
+    )
+    put(HEAD_AT + D, rest)
+    for d in range(32):
+        small_ref[d, ROWS : 2 * HALF, :] = loss_ref[...]
+
+
+VEC_AT = 8 * EROWS
+HEAD_AT = VEC_AT + 128
+
+
+def run_embed_back(d_rows, pix, weights, lead, embed, vec, g_vec, g_up, g_head, loss):
     vmem = pl.BlockSpec(memory_space=VM)
     smem = pl.BlockSpec(memory_space=pltpu.SMEM)
     return pl.pallas_call(
         embed_back_kernel,
         name="embed_bwd",
-        out_shape=(
-            jax.ShapeDtypeStruct((EROWS, D), F32),
-            jax.ShapeDtypeStruct((1, D), F32),
+        out_shape=jax.ShapeDtypeStruct((32, 2 * HALF, BLOCK), F32),
+        in_specs=[vmem, vmem, vmem, smem] + [vmem] * 6,
+        out_specs=vmem,
+        compiler_params=pltpu.CompilerParams(vmem_limit_bytes=40 * 1024 * 1024),
+    )(d_rows, pix, weights, lead, embed, vec, g_vec, g_up, g_head, loss)
+
+
+MATRICES = ((D, 3 * D), (D, D), (D, FF), (FF, D))
+SLOTS = 768
+
+
+def gather_kernel(
+    place_ref,
+    lead_ref,
+    blocks_ref,
+    left_ref,
+    mom_ref,
+    right_ref,
+    pix_ref,
+    ids_ref,
+    emb_ref,
+    vec_ref,
+    wqkv_hbm,
+    wo_hbm,
+    wup_hbm,
+    wdown_hbm,
+    turned_ref,
+    h0_ref,
+    n1_ref,
+    xp_ref,
+    a_ref,
+    stack,
+    strip_qkv,
+    strip_o,
+    strip_up,
+    strip_down,
+    recv,
+    send,
+    sib_send,
+    sib_recv,
+    strip_sem,
+):
+    place = Place()
+    place.greet()
+    mine = place.linear(place.z, place.x, place.y)
+    stack[pl.ds(mine * SHARE, SHARE)] = blocks_ref[...].astype(BF)
+
+    def between(number):
+        if number == 3:
+            embed_kernel(pix_ref, ids_ref, lead_ref, emb_ref, vec_ref, h0_ref, n1_ref, xp_ref, a_ref)
+        at = number - 12
+        if 0 <= at < 48 and at % 2 == 0:
+            i = at // 2
+            turned_ref[i] = mmh(mmh(left_ref[i], mom_ref[i]), right_ref[i])
+
+    gather_tree(
+        place,
+        MAIN,
+        GATHER_ORDER,
+        lambda i: stack.at[pl.ds(i * PIECE, PIECE)],
+        lambda n: stack.at[pl.ds(0, n * PIECE)],
+        recv,
+        send,
+        sib_send,
+        sib_recv,
+        between,
+    )
+
+    begin = 0
+    groups = (
+        (strip_qkv, wqkv_hbm),
+        (strip_o, wo_hbm),
+        (strip_up, wup_hbm),
+        (strip_down, wdown_hbm),
+    )
+    for which, ((rows, cols), (strip, target)) in enumerate(zip(MATRICES, groups)):
+        across = cols // BLOCK
+        count = rows // BLOCK
+
+        def out(r, which=which, strip=strip, target=target):
+            two = lax.rem(r, 2)
+            return pltpu.make_async_copy(
+                strip.at[two],
+                target.at[pl.ds(pl.multiple_of(r * BLOCK, BLOCK), BLOCK)],
+                strip_sem.at[which, two],
+            )
+
+        def fill(r, _, begin=begin, across=across, strip=strip, out=out):
+            @pl.when(r >= 2)
+            def _():
+                out(r - 2).wait()
+
+            two = lax.rem(r, 2)
+            for c in range(across):
+                strip[two, :, c * BLOCK : (c + 1) * BLOCK] = stack[
+                    place_ref[begin + r * across + c]
+                ]
+            out(r).start()
+            return 0
+
+        lax.fori_loop(0, count, fill, 0)
+        begin += count * across
+    for which, ((rows, cols), (strip, target)) in enumerate(zip(MATRICES, groups)):
+        count = rows // BLOCK
+        for r in (count - 2, count - 1):
+            pltpu.make_async_copy(
+                strip.at[r % 2], target.at[pl.ds(r * BLOCK, BLOCK)], strip_sem.at[which, r % 2]
+            ).wait()
+
+
+def run_gather(place, lead, blocks, left, momentum, right, pix, ids, embed, vec):
+    vmem = pl.BlockSpec(memory_space=VM)
+    smem = pl.BlockSpec(memory_space=pltpu.SMEM)
+    anyspace = pl.BlockSpec(memory_space=pl.ANY)
+    dma = pltpu.SemaphoreType.DMA
+    return pl.pallas_call(
+        gather_kernel,
+        name="gather",
+        out_shape=tuple(jax.ShapeDtypeStruct(m, BF) for m in MATRICES)
+        + (
+            jax.ShapeDtypeStruct((SHARE, BLOCK, BLOCK), F32),
+            jax.ShapeDtypeStruct((TOK, D), F32),
+            jax.ShapeDtypeStruct((TOK, D), BF),
+            jax.ShapeDtypeStruct((TOK, HOUT), F32),
+            jax.ShapeDtypeStruct((TOK, VARS), F32),
         ),
-        in_specs=[vmem, vmem, vmem, smem, vmem, vmem],
-        out_specs=(vmem,) * 2,
-    )(d_rows, pix, weights, lead, embed, vec)
+        in_specs=[smem, smem] + [vmem] * 8,
+        out_specs=(anyspace,) * 4 + (vmem,) * 5,
+        scratch_shapes=[
+            VM((SLOTS, BLOCK, BLOCK), BF),
+            VM((2, BLOCK, 3 * D), BF),
+            VM((2, BLOCK, D), BF),
+            VM((2, BLOCK, FF), BF),
+            VM((2, BLOCK, D), BF),
+            dma((4, 16)),
+            dma((4,)),
+            dma((1,)),
+            dma((1,)),
+            dma((4, 2)),
+        ],
+        compiler_params=pltpu.CompilerParams(
+            collective_id=2, has_side_effects=True, vmem_limit_bytes=60 * 1024 * 1024
+        ),
+    )(place, lead, blocks, left, momentum, right, pix, ids, embed, vec)
+
+
+ROWS = 136
+HALF = 72
+
+
+def reduce_kernel(
+    li_ref,
+    ri_ref,
+    left_hbm,
+    right_hbm,
+    small_ref,
+    lroot_ref,
+    rroot_ref,
+    own_ref,
+    ggt_ref,
+    gtg_ref,
+    lgr_ref,
+    all_ref,
+    sum_ref,
+    lt,
+    rt,
+    mine,
+    theirs,
+    acc,
+    acc_small,
+    land,
+    land_small,
+    out,
+    out_small,
+    tail,
+    in_sem,
+    swap_sem,
+    recv,
+    send,
+    recv_small,
+    send_small,
+    t_recv,
+    t_send,
+    t_sib,
+):
+    place = Place()
+    loads = [
+        pltpu.make_async_copy(left_hbm.at[0], lt.at[:, :, pl.ds(0, TOK)], in_sem.at[0]),
+        pltpu.make_async_copy(left_hbm.at[1], lt.at[:, :, pl.ds(TOK, TOK)], in_sem.at[1]),
+        pltpu.make_async_copy(right_hbm.at[0], rt.at[:, pl.ds(0, TOK), :], in_sem.at[2]),
+        pltpu.make_async_copy(right_hbm.at[1], rt.at[:, pl.ds(TOK, TOK), :], in_sem.at[3]),
+    ]
+    for c in loads:
+        c.start()
+    place.greet()
+    swap = pltpu.make_async_remote_copy(
+        small_ref.at[:, 1 - place.core],
+        theirs,
+        swap_sem.at[0],
+        swap_sem.at[1],
+        place.sibling(),
+        MESH_ID,
+    )
+    swap.start()
+    for c in loads:
+        c.wait()
+    swap.wait()
+    mine[...] = small_ref[:, place.core] + theirs[...]
+
+    def own_piece(part, device, chip, out_at):
+        if part < 4:
+
+            def block(j, _):
+                slot = device * SHARE + part * PIECE + j
+                acc[j] = mm(lt[li_ref[slot]], rt[ri_ref[slot]])
+                return 0
+
+            lax.fori_loop(0, PIECE, block, 0, unroll=3)
+        else:
+            acc_small[...] = mine[chip // 2, lax.rem(chip, 2), pl.ds((part - 4) * HALF, HALF), :]
+
+    def add_landed(part, index):
+        if part < 4:
+            acc[...] += land[index].astype(F32)
+        else:
+            acc_small[...] += land_small[index]
+
+    me = place.linear(place.z, place.x, place.y)
+
+    def keep(part, out_at, root):
+        if part < 4:
+            if root:
+                own_ref[pl.ds(part * PIECE, PIECE)] = acc[...]
+            else:
+                out[out_at] = acc[...].astype(BF)
+        elif root:
+            tail[me * 2 + part - 4] = acc_small[...]
+        else:
+            out_small[out_at] = acc_small[...]
+
+    base, _ = landing_base(MAIN)
+    base_small, _ = landing_base(SMALL)
+    for part, dx, dy, rank in REDUCE_ORDER:
+        if part < 4:
+            reduce_step(
+                place, MAIN, base, (part, dx, dy, rank), own_piece, add_landed,
+                land, recv, out, send, keep, 0,
+            )
+        else:
+            reduce_step(
+                place, SMALL, base_small, (part - 4, dx, dy, rank), own_piece, add_landed,
+                land_small, recv_small, out_small, send_small, keep, 4,
+            )
+    drain(place, MAIN, lambda n: out.at[pl.ds(0, n)], send, REDUCE_HOPS)
+    drain(place, SMALL, lambda n: out_small.at[pl.ds(0, n)], send_small, REDUCE_HOPS)
+
+    squares = jnp.zeros((BLOCK, BLOCK), F32)
+    for i in range(SHARE):
+        squares = squares + own_ref[i] * own_ref[i]
+    first = tail[me * 2]
+    second = tail[me * 2 + 1]
+    data = second[0 : ROWS - HALF]
+    norm = (
+        jnp.sum(squares, keepdims=True)
+        + jnp.sum(first * first, keepdims=True)
+        + jnp.sum(data * data, keepdims=True)
+    )
+    row = lax.broadcasted_iota(jnp.int32, (8, BLOCK), 0)
+    tail[me * 2 + 1, ROWS - HALF : HALF, :] = jnp.where(row < 4, norm, second[ROWS - HALF : HALF])
+
+    def between(number):
+        if number < SHARE:
+            g = own_ref[number]
+            ggt_ref[number] = mmh(g, g, NT)
+            gtg_ref[number] = mmh(g, g, TN)
+            lgr_ref[number] = mmh(mmh(lroot_ref[number], g), rroot_ref[number])
+
+    gather_tree(
+        place,
+        TAIL,
+        TAIL_ORDER,
+        lambda i: tail.at[i],
+        lambda n: tail.at[pl.ds(0, n)],
+        t_recv,
+        t_send,
+        t_sib.at[pl.ds(0, 1)],
+        t_sib.at[pl.ds(1, 1)],
+        between,
+    )
+    total = jnp.zeros((8, BLOCK), F32)
+    for d in range(32):
+        all_ref[d, 0:HALF, :] = tail[2 * d]
+        all_ref[d, HALF:ROWS, :] = tail[2 * d + 1, 0 : ROWS - HALF, :]
+        total = total + tail[2 * d + 1, ROWS - HALF : HALF, :]
+    sum_ref[0] = total
+    sum_ref[1] = tail[1, ROWS - HALF : HALF, :]
+
+
+def run_reduce(li, ri, left, right, small, lroots, rroots):
+    vmem = pl.BlockSpec(memory_space=VM)
+    smem = pl.BlockSpec(memory_space=pltpu.SMEM)
+    anyspace = pl.BlockSpec(memory_space=pl.ANY)
+    dma = pltpu.SemaphoreType.DMA
+    _, count = landing_base(MAIN)
+    _, count_small = landing_base(SMALL)
+    stack = jax.ShapeDtypeStruct((SHARE, BLOCK, BLOCK), F32)
+    return pl.pallas_call(
+        reduce_kernel,
+        name="reduce",
+        out_shape=(stack,) * 4
+        + (
+            jax.ShapeDtypeStruct((32, ROWS, BLOCK), F32),
+            jax.ShapeDtypeStruct((2, 8, BLOCK), F32),
+        ),
+        in_specs=[smem, smem, anyspace, anyspace, vmem, vmem, vmem],
+        out_specs=(vmem,) * 6,
+        scratch_shapes=[
+            VM((N_LEFT, BLOCK, 2 * TOK), BF),
+            VM((N_RIGHT, 2 * TOK, BLOCK), BF),
+            VM((8, 2, 2 * HALF, BLOCK), F32),
+            VM((8, 2, 2 * HALF, BLOCK), F32),
+            VM((PIECE, BLOCK, BLOCK), F32),
+            VM((HALF, BLOCK), F32),
+            VM((count, PIECE, BLOCK, BLOCK), BF),
+            VM((count_small, HALF, BLOCK), F32),
+            VM((64, PIECE, BLOCK, BLOCK), BF),
+            VM((32, HALF, BLOCK), F32),
+            VM((64, HALF, BLOCK), F32),
+            dma((4,)),
+            dma((2,)),
+            dma((count,)),
+            dma((4,)),
+            dma((count_small,)),
+            dma((4,)),
+            dma((2, 16)),
+            dma((4,)),
+            dma((2,)),
+        ],
+        compiler_params=pltpu.CompilerParams(
+            collective_id=3, has_side_effects=True, vmem_limit_bytes=60 * 1024 * 1024
+        ),
+    )(li, ri, left, right, small, lroots, rroots)
 
 
 def fast_shards(
@@ -1077,11 +1701,14 @@
     head_first,
     head_second,
 ):
-    stack = lax.all_gather(blocks.astype(BF), ("seq", "batch"), axis=0, tiled=True)
-    natural = jnp.zeros_like(stack).at[block_order].set(stack)
-    mats = split_matrices(natural)
+    slots = jnp.arange(SLOTS, dtype=jnp.int32)
+    hit = block_order[None, :] == slots[:, None]
+    place = jnp.sum(jnp.where(hit, slots[None, :], 0), 1)
     ids = (4 * var_ids[0][:, None] + jnp.arange(4, dtype=jnp.int32)[None]).reshape(HOUT, 1)
-    h0, n1, pix, weights = run_embed(inputs[0], ids, lead_ids, embed_params, vectors)
+    *mats, turned, h0, n1, pix, weights = run_gather(
+        place, lead_ids, blocks, left_roots, block_momentum, right_roots,
+        inputs[0], ids, embed_params, vectors,
+    )
     bias = jnp.concatenate([vectors[9], jnp.zeros_like(vectors[9]), vectors[10]])[None]
     bup = vectors[11:].reshape(1, FF)
     nlat = 2 * LAT_P
@@ -1094,42 +1721,33 @@
     left, right, d_rows, g_vec, g_up, g_head, loss = run_layer(
         n1, h0, vectors, bias, bup, targets[0], head_weight.astype(BF), wlat, mats
     )
-    g_embed, g_query = run_embed_back(d_rows, pix, weights, lead_ids, embed_params, vectors)
-    g_vectors = jnp.concatenate([g_query, g_vec[1:11], g_up.reshape(-1, D)])
-    pairs = ((0, 8, 0, 24), (8, 16, 24, 32), (16, 24, 32, 64), (24, 56, 64, 72))
-    grads = jnp.concatenate(
-        [
-            jnp.einsum(
-                "rit,ctj->rcij", left[0, a:e], right[0, f:g], preferred_element_type=F32
-            ).reshape(-1, BLOCK, BLOCK)
-            for a, e, f, g in pairs
-        ]
-    )
-    owned = lax.psum_scatter(
-        grads[block_order], ("seq", "batch"), scatter_dimension=0, tiled=True
-    )
-    g_embed, g_vectors, g_head, loss_total = lax.psum(
-        (g_embed, g_vectors, g_head, loss[0, 0]), ("seq", "batch")
-    )
-    rest_squares = (
-        jnp.sum(g_embed * g_embed) + jnp.sum(g_vectors * g_vectors) + jnp.sum(g_head * g_head)
-    )
-    grad_norm = jnp.sqrt(lax.psum(jnp.sum(owned * owned), ("seq", "batch")) + rest_squares)
+    small = run_embed_back(
+        d_rows, pix, weights, lead_ids, embed_params, vectors, g_vec, g_up, g_head, loss
+    )
+    o = block_order
+    li = jnp.where(
+        o < 192, o // 24, jnp.where(o < 256, o // 8 - 16, jnp.where(o < 512, o // 32 + 8, o // 8 - 40))
+    )
+    ri = jnp.where(
+        o < 192, o % 24, jnp.where(o < 256, 24 + o % 8, jnp.where(o < 512, 32 + o % 32, 64 + o % 8))
+    )
+    owned, ggt, gtg, lgr, every, sums = run_reduce(
+        li, ri, left, right, small.reshape(8, 2, 2, 2 * HALF, BLOCK), left_roots, right_roots
+    )
+    flat = every.reshape(32 * ROWS, BLOCK)
+    g_embed = flat[:VEC_AT].reshape(8, EROWS, BLOCK).transpose(1, 0, 2).reshape(EROWS, D)
+    g_vectors = flat[VEC_AT:HEAD_AT].reshape(8, 16, BLOCK).transpose(1, 0, 2).reshape(16, D)[:15]
+    g_head = jnp.concatenate(
+        [flat[HEAD_AT : HEAD_AT + D], flat[HEAD_AT + D :, : HOUT - BLOCK]], 1
+    )
+    loss_total = sums[1, 4, 0]
+    grad_norm = jnp.sqrt(sums[0, 0, 0])
     clip = CLIP_NORM / jnp.maximum(grad_norm, CLIP_NORM)
-    owned = owned * clip
-    new_momentum = BETA_ONE * block_momentum + (1.0 - BETA_ONE) * owned
-    new_left = BETA_TWO * left_stats + (1.0 - BETA_TWO) * jnp.einsum(
-        "bij,bkj->bik", owned, owned, precision=HIGH
-    )
-    new_right = BETA_TWO * right_stats + (1.0 - BETA_TWO) * jnp.einsum(
-        "bji,bjk->bik", owned, owned, precision=HIGH
-    )
-    direction = jnp.einsum(
-        "bij,bjk->bik",
-        jnp.einsum("bij,bjk->bik", left_roots, new_momentum, precision=HIGH),
-        right_roots,
-        precision=HIGH,
-    )
+    scaled = owned * clip
+    new_momentum = BETA_ONE * block_momentum + (1.0 - BETA_ONE) * scaled
+    new_left = BETA_TWO * left_stats + ((1.0 - BETA_TWO) * clip) * (ggt * clip)
+    new_right = BETA_TWO * right_stats + ((1.0 - BETA_TWO) * clip) * (gtg * clip)
+    direction = BETA_ONE * turned + ((1.0 - BETA_ONE) * clip) * lgr
     new_blocks = blocks - SHAMPOO_RATE * (direction + DECAY * blocks)
     e_one, e_two, e_new = adam(embed_params, embed_first, embed_second, g_embed * clip, EMBED_RATE)
     v_one, v_two, v_new = adam(vectors, vector_first, vector_second, g_vectors * clip, VECTOR_RATE)

time: 1250 us -> 439 us (0.35)
  waiting for transfers between devices: 641 us -> 0 us
  local copies, waits for them, and re-layouts: 321 us -> 17.7 us
  Pallas kernels: 127 us -> 389 us
  matrix products: 43.1 us -> 0 us
  blocking collectives: 40 us -> 0 us
  other arithmetic: 56 us -> 21.4 us
  between operations: 19.7 us -> 4.28 us
    reduce_scatter x1 -> x0, waiting for transfers between devices: 434 us -> none  [fast_shards(): lax.psum_scatter(grads[block_order], ('seq', 'batch'), scatter_dimension=...]
    pallas_call x2 -> x3, Pallas kernels: 9.93 us -> 271 us  [the longest x1 142 us: run_reduce(): pl.pallas_call(reduce_kernel, name='reduce', out_shape=(stack,) * 4 + (ja...]
    all_gather x1 -> x0, waiting for transfers between devices: 145 us -> none  [fast_shards(): lax.all_gather(blocks.astype(BF), ('seq', 'batch'), axis=0, tiled=True)]
    scatter x1 -> x0, local copies, waits for them, and re-layouts: 112 us -> none  [fast_shards(): natural = jnp.zeros_like(stack).at[block_order].set(stack)]
    transpose x8 -> x0, local copies, waits for them, and re-layouts: 94.3 us -> none  [the longest x4 53.1 us: fast_shards(): jnp.einsum('rit,ctj->rcij', left[0, a:e], right[0, f:g], preferred_elemen...]
    psum x1 -> x0, waiting for transfers between devices: 61.5 us -> none  [fast_shards(): lax.psum((g_embed, g_vectors, g_head, loss[0, 0]), ('seq', 'batch'))]
    dot_general x8 -> x0, matrix products: 43.1 us -> none  [the longest x4 30 us: fast_shards(): jnp.einsum('rit,ctj->rcij', left[0, a:e], right[0, f:g], preferred_elemen...]
    psum x1 -> x0, blocking collectives: 40 us -> none  [fast_shards(): lax.psum((g_embed, g_vectors, g_head, loss[0, 0]), ('seq', 'batch'))]
  transfers between devices with their start and end apart: 3 -> 0, of which waited for: 3 -> 0; matrix products, arithmetic and copies ran while one was open for 7% -> 0% of each run, Pallas kernels for 0% -> 0%
where the time goes in v2:
time: 439 us; the launch traced here: 432 us
  Pallas kernels  389 us (89%)
  other arithmetic  21.4 us (5%)
  local copies, waits for them, and re-layouts  17.7 us (4%)
    pallas_call x1, Pallas kernels, run_reduce(): pl.pallas_call(reduce_kernel, name='reduce', out_shape=(stack,) * 4 + (ja...  142 us
    pallas_call x1, Pallas kernels, run_gather(): pl.pallas_call(gather_kernel, name='gather', out_shape=tuple((jax.ShapeDt...  126 us
    pallas_call x1, Pallas kernels, run_layer(): pl.pallas_call(layer_kernel, name='layer', out_shape=(jax.ShapeDtypeStruc...  118 us
    unnamed x48, local copies, waits for them, and re-layouts  10.8 us

profile of v2, /device:TPU:0, one launch (start us, length us, event | category | flops | bytes accessed | tf_op | source)
XLA Modules:
  0.0 432.2 jit_solution(5703559345741906534)
XLA Ops:
  2.0 0.7 add.175.ids_ref
  2.8 1.5 copy.60
  4.3 1.6 select_reduce_fusion.place_ref
  5.9 126.1 %gather.1 = (bf16[1024,3072]{1,0:T(8,128)(2,1)}, bf16[1024,1024]{1,0:T(8,128)(2,1)}, bf16[1024,4096]{1,0:T(8,128)(2,1)}, bf16[4096,1024]{1,0:T(8,128)(2,1)}, f32...) custom-call(s32[768]{0:T(1024)} %select_reduce_fusion.place_ref, ...), custom_call_target="tpu_custom_call" | custom-call | tf_op jit(solution)/shard_map/gather/pallas_call | solution.py:1453
  132.0 0.8 fusion.19
  133.5 1.0 copy.63.head_ref
  136.1 0.8 copy.64.wlat_ref
  136.8 0.7 copy.62
  137.6 0.8 slice_bitcast_fusion
  138.9 117.8 %layer.1 = (bf16[2,56,128,128]{3,2,1,0:T(8,128)(2,1)}, bf16[2,72,128,128]{3,2,1,0:T(8,128)(2,1)}, f32[128,1024]{1,0:T(8,128)}, f32[16,1024]{1,0:T(8,128)}, f32[1...) custom-call(bf16[128,1024]{1,0:T(8,128)(2,1)} %get-tuple-element.37.n1_ref, ...), custom_call_target="tpu_custom_call" | custom-call | tf_op jit(solution)/shard_map/layer/pallas_call | solution.py:1184
  256.8 1.2 copy-done.3
  258.0 1.0 copy-done.4
  259.1 0.8 copy-done.7
  259.9 0.7 copy-done.8
  261.3 3.3 embed_bwd.1
  264.6 1.4 copy-done.1
  266.7 141.6 %reduce.1 = (f32[24,128,128]{2,1,0:T(8,128)}, f32[24,128,128]{2,1,0:T(8,128)}, f32[24,128,128]{2,1,0:T(8,128)}, f32[24,128,128]{2,1,0:T(8,128)}, f32[32,136,128]{2,1,0:T(8,128)}, /*index=5*/f32[2,8,128]{2,1,0:T(8,128)}) custom-call(s32[768]{0:T(1024)} %get-tuple-element.73.li_ref, s32[768]{0:T(1024)} %get-tuple-element.72.ri_ref, ...), custom_call_target="tpu_custom_call" | custom-call | tf_op jit(solution)/shard_map/reduce/pallas_call | solution.py:1644
  408.3 1.1 slice.44
  409.6 1.1 slice.45
  410.8 1.2 fusion.20
  412.8 3.3 multiply_subtract_fusion.2
  417.8 2.5 multiply_subtract_fusion.1
  420.3 5.6 %multiply_add_fusion = (f32[24,128,128]{2,1,0:T(8,128)}, f32[24,128,128]{2,1,0:T(8,128)}) fusion(f32[24,128,128]{2,1,0:T(8,128)} %get-tuple-element.57, f32[24,128,128]{2,1,0:T(8,128)} %param.28, f32[]{:T(128)S(6)} %mul.249, f32[]{:T(128)S(6)} %div.115, f32[24,128,128]{2,1,0:T(8,128)} %get-tuple-element.56, f32[24,128,128]{2,1,0:T(8,128)} %param.27), kind=kLoop, calls=%fused_computation.3 | loop fusion | flops 3145728 | bytes 9437192 | tf_op jit(solution)/shard_map/add | solution.py:1749
  425.9 4.9 %multiply_add_fusion.2 = (f32[24,128,128]{2,1,0:T(8,128)}, f32[24,128,128]{2,1,0:T(8,128)}) fusion(f32[24,128,128]{2,1,0:T(8,128)} %get-tuple-element.55, f32[24,128,128]{2,1,0:T(8,128)S(1)} %copy-done.11, f32[]{:T(128)S(6)} %div.115, f32[24,128,128]{2,1,0:T(8,128)S(1)} %copy-done.10, f32[24,128,128]{2,1,0:T(8,128)} %get-tuple-element.54, f32[]{:T(128)S(6)} %mul.238, ...), kind=kLoop, calls=%fused_computation.5 | loop fusion | flops 4325376 | bytes 11010056 | tf_op jit(solution)/shard_map/add | solution.py:1747
  (55 shorter events, 6.3 us)
Async XLA Ops:
  5.9 127.5 %copy-start.12 = (f32[1024,192]{0,1:T(8,128)S(1)}, f32[1024,192]{0,1:T(8,128)}, u32[]{:S(2)}) copy-start(f32[1024,192]{0,1:T(8,128)} %param.37) | copy-start | bytes 2359300
  131.9 4.9 %copy-start.18 = (bf16[1,128,192]{1,2,0:T(8,128)(2,1)S(1)}, bf16[1,128,192]{1,2,0:T(8,128)(2,1)}, u32[]{:S(2)}) copy-start(bf16[1,128,192]{1,2,0:T(8,128)(2,1)} %param.21) | copy-start | bytes 147460
  138.9 117.8 %copy-start = (f32[272,1024]{1,0:T(8,128)S(1)}, f32[272,1024]{1,0:T(8,128)}, u32[]{:S(2)}) copy-start(f32[272,1024]{1,0:T(8,128)} %emb_ref.3) | copy-start | bytes 3342340
  138.9 117.8 %copy-start.2 = (f32[15,1024]{1,0:T(8,128)S(1)}, f32[15,1024]{1,0:T(8,128)}, u32[]{:S(2)}) copy-start(f32[15,1024]{1,0:T(8,128)} %vec_ref.5) | copy-start | bytes 184324
  138.9 117.8 %copy-start.5 = (f32[128,192]{1,0:T(8,128)S(1)}, f32[128,192]{1,0:T(8,128)}, u32[]{:S(2)}) copy-start(f32[128,192]{1,0:T(8,128)} %get-tuple-element.46.xp_ref) | copy-start | bytes 294916
  138.9 117.8 %copy-start.6 = (f32[128,48]{1,0:T(8,128)S(1)}, f32[128,48]{1,0:T(8,128)}, u32[]{:S(2)}) copy-start(f32[128,48]{1,0:T(8,128)} %get-tuple-element.47.a_ref) | copy-start | bytes 73732
  256.8 1.2 copy-start.3
  258.0 1.0 copy-start.4
  259.1 0.8 copy-start.7
  259.9 0.7 copy-start.8
  260.6 0.7 copy-start.9
  261.3 4.8 %copy-start.19 = (s32[768]{0:T(1024)S(1)}, s32[768]{0:T(1024)}, u32[]{:S(2)}) copy-start(s32[768]{0:T(1024)} %param.24) | copy-start | bytes 9220
  264.6 1.4 copy-start.1
  412.8 3.4 copy-start.13
  412.8 3.5 copy-start.16
  412.8 3.5 copy-start.17
  416.2 1.3 copy-start.14
  416.2 1.6 copy-start.15
  420.3 5.6 %copy-start.10 = (f32[24,128,128]{2,1,0:T(8,128)S(1)}, f32[24,128,128]{2,1,0:T(8,128)}, u32[]{:S(2)}) copy-start(f32[24,128,128]{2,1,0:T(8,128)} %blocks_ref.1) | copy-start | bytes 4718596
  420.3 5.6 %copy-start.11 = (f32[24,128,128]{2,1,0:T(8,128)S(1)}, f32[24,128,128]{2,1,0:T(8,128)}, u32[]{:S(2)}) copy-start(f32[24,128,128]{2,1,0:T(8,128)} %mom_ref.1) | copy-start | bytes 4718596
